TPU v7x, 32 devices: a whole 2x2x4 slice. The times are simulated.
32 devices in a mesh: fsdp: 4 (over z), rep: 8 (over y, x, core).
Axes of the slice: x: 2, y: 2, z: 4, core: 2. Of those that a mesh axis runs over, the one named last changes fastest.
Arguments:
- embedded: bfloat16 [2, 32, 384, 768], P(None, ('fsdp', 'rep')), may hold values from -6 to 6
- cotangent: bfloat16 [2, 32, 384, 768], P(None, ('fsdp', 'rep')), may hold values from -6 to 6
- ngram_ids: int32 [2, 2, 32, 384], P(None, None, ('fsdp', 'rep')), may hold values from 0 to 7167
- segments: int32 [2, 32, 384], P(None, ('fsdp', 'rep')), may hold values from 0 to 2, never falling along the last dimension, each value on 1 to 192 neighbouring positions
- live_mask: int32 [2, 32, 384], P(None, ('fsdp', 'rep')), may hold values from 0 to 1, as said below
- tables: bfloat16 [2, 7168, 192], P(None, 'fsdp'), may hold values from -6 to 6
- w_qkv: bfloat16 [768, 2304], P('fsdp'), may hold values from -0.21875 to 0.21875
- w_out: bfloat16 [768, 768], P('fsdp'), may hold values from -0.875 to 0.875
- w_gate_up: bfloat16 [768, 4096], P('fsdp'), may hold values from -0.21875 to 0.21875
- w_down: bfloat16 [2048, 768], P('fsdp'), may hold values from -0.125 to 0.125
- up_proj: bfloat16 [384, 768], P('fsdp'), may hold values from -0.3125 to 0.3125
- norm_gains: bfloat16 [2, 768], P(None, 'fsdp'), may hold values from 0.5 to 1.5
Outputs:
- output: bfloat16 [2, 32, 384, 768], P(None, ('fsdp', 'rep'))
- embedding_grad: bfloat16 [2, 32, 384, 768], P(None, ('fsdp', 'rep'))
- table_grad: float32 [2, 7168, 192], P(None, 'fsdp')
- qkv_grad: float32 [768, 2304], P('fsdp')
- out_grad: float32 [768, 768], P('fsdp')
- gate_up_grad: float32 [768, 4096], P('fsdp')
- down_grad: float32 [2048, 768], P('fsdp')
- up_grad: float32 [384, 768], P('fsdp')
- gains_grad: float32 [2, 768], P(None, 'fsdp')
Inputs may be any that keep to these rules, and one draw needn't show every extreme that they name: `segments`: segment numbers never fall along a sequence; every sequence holds 3 documents of 1 to 192 positions, one of exactly 192. `live_mask`: in each sequence the real tokens come first and the padding last; at most 96 positions of a sequence are padding, and some sequence has exactly that many.
All inputs are finite; a program needn't handle non-finite values.
Results may differ from a plain program's by a relative error of at most 0.015.
Values may be sent and summed in bfloat16 or wider, within the bound.
No kernel may reach another device: no remote copies, remote signals or barrier semaphores. Data moves between devices by JAX's collectives and lax.ppermute only.
A program may use at most 192 MiB of HBM per device.

v0:
```python
import jax
import jax.numpy as jnp
from jax import lax
from jax.sharding import PartitionSpec as P

HEADS = 12
HEAD_DIM = 64
FF = 2048


norm_eps = 1e-05
theta_base = 10000.0
masked_score = -1e30


def rotary_tables(segment, head_dim):
    seq_len = segment.shape[0]
    position_ids = jnp.arange(seq_len, dtype=jnp.int32)
    boundary = jnp.concatenate([jnp.ones((1,), dtype=bool), segment[1:] != segment[:-1]])
    starts = lax.cummax(jnp.where(boundary, position_ids, 0), axis=0)
    offsets = (position_ids - starts).astype(jnp.float32)
    half_dim = head_dim // 2
    frequency = theta_base ** (-jnp.arange(half_dim, dtype=jnp.float32) / half_dim)
    angles = offsets[:, None] * frequency[None, :]
    return (jnp.cos(angles), jnp.sin(angles))


def rotate(stacked, cosine_table, sine_table):
    half_dim = stacked.shape[-1] // 2
    low_half = stacked[..., :half_dim]
    high_half = stacked[..., half_dim:]
    cosine_table = cosine_table[:, None, :]
    sine_table = sine_table[:, None, :]
    return jnp.concatenate(
        [
            low_half * cosine_table - high_half * sine_table,
            high_half * cosine_table + low_half * sine_table,
        ],
        axis=-1,
    )


def rotate_back(gradient, cosine_table, sine_table):
    half_dim = gradient.shape[-1] // 2
    low_half = gradient[..., :half_dim]
    high_half = gradient[..., half_dim:]
    cosine_table = cosine_table[:, None, :]
    sine_table = sine_table[:, None, :]
    return jnp.concatenate(
        [
            low_half * cosine_table + high_half * sine_table,
            high_half * cosine_table - low_half * sine_table,
        ],
        axis=-1,
    )


def usable_keys(segment, live_row):
    seq_len = segment.shape[0]
    position_ids = jnp.arange(seq_len, dtype=jnp.int32)
    same_doc = segment[:, None] == segment[None, :]
    causal = position_ids[None, :] <= position_ids[:, None]
    diagonal = position_ids[None, :] == position_ids[:, None]
    return same_doc & causal & (live_row[None, :] == 1) | diagonal


def masked_scores(queries, key_rows, usable):
    scores = (
        jnp.einsum("qhd,khd->hqk", queries, key_rows, preferred_element_type=jnp.float32) * 0.125
    )
    return jnp.where(usable[None], scores, masked_score)


def forward_sequence(embedded, gram_rows, weights, segment, live_row):
    w_qkv, w_out, w_gate_up, w_down, up_proj, norm_gains = weights
    seq_len, model_width = embedded.shape
    gain_rows = norm_gains.astype(jnp.float32)
    residual = embedded.astype(jnp.float32) + jnp.dot(
        gram_rows, up_proj, preferred_element_type=jnp.float32
    )
    inverse_one = lax.rsqrt(jnp.mean(residual * residual, axis=-1, keepdims=True) + norm_eps)
    normed_one = residual * inverse_one
    act_one = (normed_one * gain_rows[0]).astype(jnp.bfloat16)
    projected = jnp.dot(act_one, w_qkv, preferred_element_type=jnp.float32)
    cosine_table, sine_table = rotary_tables(segment, HEAD_DIM)
    queries = rotate(
        projected[:, :model_width].reshape(seq_len, HEADS, HEAD_DIM), cosine_table, sine_table
    ).astype(jnp.bfloat16)
    key_rows = rotate(
        projected[:, model_width : 2 * model_width].reshape(seq_len, HEADS, HEAD_DIM),
        cosine_table,
        sine_table,
    ).astype(jnp.bfloat16)
    values = projected[:, 2 * model_width :].reshape(seq_len, HEADS, HEAD_DIM).astype(jnp.bfloat16)
    usable = usable_keys(segment, live_row)
    scores = masked_scores(queries, key_rows, usable)
    row_max = jnp.max(scores, axis=-1, keepdims=True)
    exp_scores = jnp.exp(scores - row_max)
    exp_total = jnp.sum(exp_scores, axis=-1, keepdims=True)
    probability = exp_scores / exp_total
    log_total = row_max + jnp.log(exp_total)
    attended = jnp.einsum(
        "hqk,khd->qhd", probability.astype(jnp.bfloat16), values, preferred_element_type=jnp.float32
    )
    attended = attended.reshape(seq_len, model_width).astype(jnp.bfloat16)
    residual_mid = residual + jnp.dot(attended, w_out, preferred_element_type=jnp.float32)
    inverse_two = lax.rsqrt(
        jnp.mean(residual_mid * residual_mid, axis=-1, keepdims=True) + norm_eps
    )
    normed_two = residual_mid * inverse_two
    act_two = (normed_two * gain_rows[1]).astype(jnp.bfloat16)
    gate_up = jnp.dot(act_two, w_gate_up, preferred_element_type=jnp.float32)
    gate_part = gate_up[:, :FF]
    inner_act = (gate_part * jax.nn.sigmoid(gate_part) * gate_up[:, FF:]).astype(jnp.bfloat16)
    output = (residual_mid + jnp.dot(inner_act, w_down, preferred_element_type=jnp.float32)).astype(
        jnp.bfloat16
    )
    saved_state = (
        gram_rows,
        normed_one,
        inverse_one,
        act_one,
        queries,
        key_rows,
        values,
        usable,
        log_total,
        attended,
        normed_two,
        inverse_two,
        act_two,
        gate_up,
        inner_act,
        cosine_table,
        sine_table,
    )
    return (output, saved_state)


def norm_back(grad_act, normed, inverse, gain_row):
    gain_grad = jnp.sum(grad_act * normed, axis=0)
    grad_normed = grad_act * gain_row
    grad_input = inverse * (
        grad_normed - normed * jnp.mean(grad_normed * normed, axis=-1, keepdims=True)
    )
    return (gain_grad, grad_input)


def backward_sequence(cotangent, weights, saved_state):
    w_qkv, w_out, w_gate_up, w_down, up_proj, norm_gains = weights
    (
        gram_rows,
        normed_one,
        inverse_one,
        act_one,
        queries,
        key_rows,
        values,
        usable,
        log_total,
        attended,
        normed_two,
        inverse_two,
        act_two,
        gate_up,
        inner_act,
        cosine_table,
        sine_table,
    ) = saved_state
    seq_len, model_width = cotangent.shape
    gain_rows = norm_gains.astype(jnp.float32)
    down_part = jnp.einsum("tf,td->fd", inner_act, cotangent, preferred_element_type=jnp.float32)
    grad_inner = jnp.einsum("td,fd->tf", cotangent, w_down, preferred_element_type=jnp.float32)
    gate_part = gate_up[:, :FF]
    up_part = gate_up[:, FF:]
    sigmoid_gate = jax.nn.sigmoid(gate_part)
    grad_gate = grad_inner * up_part * (sigmoid_gate * (1.0 + gate_part * (1.0 - sigmoid_gate)))
    grad_up = grad_inner * gate_part * sigmoid_gate
    grad_gate_up = jnp.concatenate([grad_gate, grad_up], axis=-1).astype(jnp.bfloat16)
    gate_up_part = jnp.einsum(
        "td,tf->df", act_two, grad_gate_up, preferred_element_type=jnp.float32
    )
    grad_act_two = jnp.einsum(
        "tf,df->td", grad_gate_up, w_gate_up, preferred_element_type=jnp.float32
    )
    gain_two_part, grad_norm_two = norm_back(grad_act_two, normed_two, inverse_two, gain_rows[1])
    grad_mid = cotangent.astype(jnp.float32) + grad_norm_two
    grad_mid_low = grad_mid.astype(jnp.bfloat16)
    out_part = jnp.einsum("td,te->de", attended, grad_mid_low, preferred_element_type=jnp.float32)
    grad_attended = jnp.einsum("te,de->td", grad_mid_low, w_out, preferred_element_type=jnp.float32)
    grad_attended = grad_attended.astype(jnp.bfloat16).reshape(seq_len, HEADS, HEAD_DIM)
    probability = jnp.exp(masked_scores(queries, key_rows, usable) - log_total)
    grad_probability = jnp.einsum(
        "qhd,khd->hqk", grad_attended, values, preferred_element_type=jnp.float32
    )
    row_dot = jnp.sum(grad_probability * probability, axis=-1, keepdims=True)
    grad_scores = (probability * (grad_probability - row_dot)).astype(jnp.bfloat16)
    grad_values = jnp.einsum(
        "hqk,qhd->khd",
        probability.astype(jnp.bfloat16),
        grad_attended,
        preferred_element_type=jnp.float32,
    )
    grad_queries = (
        jnp.einsum("hqk,khd->qhd", grad_scores, key_rows, preferred_element_type=jnp.float32)
        * 0.125
    )
    grad_keys = (
        jnp.einsum("hqk,qhd->khd", grad_scores, queries, preferred_element_type=jnp.float32) * 0.125
    )
    grad_projected = jnp.concatenate(
        [
            rotate_back(grad_queries, cosine_table, sine_table).reshape(seq_len, model_width),
            rotate_back(grad_keys, cosine_table, sine_table).reshape(seq_len, model_width),
            grad_values.reshape(seq_len, model_width),
        ],
        axis=-1,
    ).astype(jnp.bfloat16)
    qkv_part = jnp.einsum("td,te->de", act_one, grad_projected, preferred_element_type=jnp.float32)
    grad_act_one = jnp.einsum(
        "te,de->td", grad_projected, w_qkv, preferred_element_type=jnp.float32
    )
    gain_one_part, grad_norm_one = norm_back(grad_act_one, normed_one, inverse_one, gain_rows[0])
    embedding_grad = (grad_mid + grad_norm_one).astype(jnp.bfloat16)
    up_part_grad = jnp.einsum(
        "tr,td->rd", gram_rows, embedding_grad, preferred_element_type=jnp.float32
    )
    grad_rows = jnp.einsum(
        "td,rd->tr", embedding_grad, up_proj, preferred_element_type=jnp.float32
    ).astype(jnp.bfloat16)
    gains_part = jnp.stack([gain_one_part, gain_two_part])
    return (
        embedding_grad,
        grad_rows,
        (qkv_part, out_part, gate_up_part, down_part, up_part_grad, gains_part),
    )


def add_rows(table_total, group_rows, clipped_ids, owned_mask, emb_width):
    for table_slot in range(2):
        piece = group_rows[..., table_slot * emb_width : (table_slot + 1) * emb_width].astype(
            jnp.float32
        )
        contribution = jnp.where(owned_mask[table_slot][..., None], piece, 0.0).reshape(
            -1, emb_width
        )
        table_total = table_total.at[table_slot, clipped_ids[table_slot].reshape(-1)].add(
            contribution
        )
    return table_total


def body(
    embedded,
    cotangent,
    ngram_ids,
    segments,
    live_mask,
    tables,
    w_qkv,
    w_out,
    w_gate_up,
    w_down,
    up_proj,
    norm_gains,
):
    micro_total = embedded.shape[0]
    rows_dev = tables.shape[1]
    emb_width = tables.shape[2]
    owner_index = lax.axis_index("fsdp")
    group_ids = lax.all_gather(ngram_ids, "fsdp", axis=2, tiled=True)
    local_ids = group_ids - owner_index * rows_dev
    owned_mask = (local_ids >= 0) & (local_ids < rows_dev)
    clipped = jnp.clip(local_ids, 0, rows_dev - 1)
    kept_full = (
        lax.all_gather(w_qkv, "fsdp", axis=0, tiled=True),
        lax.all_gather(w_out, "fsdp", axis=0, tiled=True),
        lax.all_gather(w_gate_up, "fsdp", axis=0, tiled=True),
        lax.all_gather(w_down, "fsdp", axis=0, tiled=True),
        lax.all_gather(up_proj, "fsdp", axis=0, tiled=True),
        lax.all_gather(norm_gains, "fsdp", axis=1, tiled=True),
    )
    shard_list = (w_qkv, w_out, w_gate_up, w_down, up_proj, norm_gains)
    weight_totals = tuple((jnp.zeros(shard.shape, jnp.float32) for shard in shard_list))
    table_total = jnp.zeros(tables.shape, jnp.float32)
    outputs = []
    emb_grads = []
    for batch_index in range(micro_total):
        picked = jnp.concatenate(
            [
                jnp.where(
                    owned_mask[table_slot, batch_index][..., None],
                    tables[table_slot][clipped[table_slot, batch_index]],
                    0.0,
                )
                for table_slot in range(2)
            ],
            axis=-1,
        ).astype(jnp.float32)
        gram_rows = lax.psum_scatter(
            picked.astype(jnp.bfloat16), "fsdp", scatter_dimension=0, tiled=True
        )[0]
        output, saved_state = forward_sequence(
            embedded[batch_index, 0],
            gram_rows,
            kept_full,
            segments[batch_index, 0],
            live_mask[batch_index, 0],
        )
        outputs.append(output)
        embedding_grad, grad_rows, weight_parts = backward_sequence(
            cotangent[batch_index, 0], kept_full, saved_state
        )
        emb_grads.append(embedding_grad)
        group_rows = lax.all_gather(grad_rows[None], "fsdp", axis=0, tiled=True)
        table_total = add_rows(
            table_total, group_rows, clipped[:, batch_index], owned_mask[:, batch_index], emb_width
        )
        qkv_part, out_part, gate_up_part, down_part, up_part_grad, gains_part = weight_parts
        grad_shards = (
            lax.psum_scatter(qkv_part, "fsdp", scatter_dimension=0, tiled=True),
            lax.psum_scatter(out_part, "fsdp", scatter_dimension=0, tiled=True),
            lax.psum_scatter(gate_up_part, "fsdp", scatter_dimension=0, tiled=True),
            lax.psum_scatter(down_part, "fsdp", scatter_dimension=0, tiled=True),
            lax.psum_scatter(up_part_grad, "fsdp", scatter_dimension=0, tiled=True),
            lax.psum_scatter(gains_part, "fsdp", scatter_dimension=1, tiled=True),
        )
        weight_totals = tuple((total + part for total, part in zip(weight_totals, grad_shards)))
    summed = lax.psum(
        (
            weight_totals[0],
            weight_totals[1],
            weight_totals[2],
            weight_totals[3],
            weight_totals[4],
            weight_totals[5],
            table_total,
        ),
        "rep",
    )
    output_all = jnp.stack(outputs)[:, None]
    emb_grad_all = jnp.stack(emb_grads)[:, None]
    return (
        output_all,
        emb_grad_all,
        summed[6],
        summed[0],
        summed[1],
        summed[2],
        summed[3],
        summed[4],
        summed[5],
    )


def solution(mesh):
    in_specs = (
        P(None, ("fsdp", "rep"), None, None),
        P(None, ("fsdp", "rep"), None, None),
        P(None, None, ("fsdp", "rep"), None),
        P(None, ("fsdp", "rep"), None),
        P(None, ("fsdp", "rep"), None),
        P(None, "fsdp", None),
        P("fsdp", None),
        P("fsdp", None),
        P("fsdp", None),
        P("fsdp", None),
        P("fsdp", None),
        P(None, "fsdp"),
    )
    out_specs = (
        P(None, ("fsdp", "rep"), None, None),
        P(None, ("fsdp", "rep"), None, None),
        P(None, "fsdp", None),
        P("fsdp", None),
        P("fsdp", None),
        P("fsdp", None),
        P("fsdp", None),
        P("fsdp", None),
        P(None, "fsdp"),
    )
    return jax.shard_map(body, mesh=mesh, in_specs=in_specs, out_specs=out_specs, check_vma=False)
```

profile of v0, /device:TPU:13, one launch (start us, length us, event | category | flops | bytes accessed | tf_op | source)
XLA Modules:
  0.0 1257.7 jit_solution(16682202774064393055)
XLA Ops:
  7.9 10.4 all_gather.27
  21.1 4.8 gather_fusion.3
  26.4 4.8 gather_fusion.2
  33.1 4.8 gather_fusion.1
  37.9 4.8 gather_fusion
  47.5 22.3 %all_gather.28 = bf16[384,768]{1,0:T(8,128)(2,1)S(1)} all-gather(bf16[96,768]{1,0:T(8,128)(2,1)S(1)} %copy-done.84), channel_id=1, replica_groups=mesh['fsdp'=4,'rep'=8] {'fsdp'}, dimensions={0}, use_global_device_ids=true | all-gather | bytes 737280 | tf_op jit(solution)/shard_map/all_gather | solution.py:280
  69.8 7.0 all-gather.2
  80.5 23.9 %reduce-scatter.11.cloned.1.call-done = bf16[1,384,384]{2,1,0:T(8,128)(2,1)} async-done(((bf16[4,384,384]{2,1,0:T(8,128)(2,1)}), bf16[1,384,384]{2,1,0:T(8,128)(2,1)}) %reduce-scatter.11.cloned.1.call-update) | async-done | bytes 294928 | tf_op jit(solution)/shard_map/reduce_scatter | solution.py:300
  106.1 68.2 %all-gather.10.cloned.1.call-done = bf16[768,2304]{1,0:T(8,128)(2,1)} async-done(((bf16[192,2304]{1,0:T(8,128)(2,1)}), bf16[768,2304]{1,0:T(8,128)(2,1)}) %all-gather.10.cloned.1.call-update) | async-done | bytes 3538960 | tf_op jit(solution)/shard_map/all_gather | solution.py:276
  174.4 3.6 fusion.93
  217.2 103.2 %all-gather.14.cloned.1.call-done = bf16[768,4096]{1,0:T(8,128)(2,1)} async-done(((bf16[192,4096]{1,0:T(8,128)(2,1)}), bf16[768,4096]{1,0:T(8,128)(2,1)}) %all-gather.14.cloned.1.call-update) | async-done | bytes 6291472 | tf_op jit(solution)/shard_map/all_gather | solution.py:278
  320.4 7.6 fusion.94
  328.0 4.5 fusion.92
  332.6 51.4 %all-gather.16.cloned.1.call-done = bf16[2048,768]{1,0:T(8,128)(2,1)} async-done(((bf16[512,768]{1,0:T(8,128)(2,1)}), bf16[2048,768]{1,0:T(8,128)(2,1)}) %all-gather.16.cloned.1.call-update) | async-done | bytes 3145744 | tf_op jit(solution)/shard_map/all_gather | solution.py:279
  384.0 7.5 multiply_convert_fusion.3
  391.6 4.2 multiply_convert_fusion.5
  398.5 3.5 multiply_reduce_fusion.4
  407.6 5.4 fusion.25
  413.0 8.0 multiply_reduce_fusion.1
  420.9 4.4 multiply_convert_fusion.1
  425.4 2.8 fusion.20
  434.0 5.4 fusion.28
  439.4 8.0 multiply_reduce_fusion
  447.4 4.4 multiply_convert_fusion
  462.5 2.9 multiply_reduce_fusion.3
  479.9 3.5 fusion.39
  483.5 4.7 convolution_add_fusion.2
  489.2 3.9 fusion.34
  493.1 5.1 convolution_add_fusion.1
  499.5 5.6 fusion.13
  505.1 6.8 convolution_add_fusion
  514.3 3.2 convert_select_fusion.2
  517.5 12.1 all-gather.20.cloned.1.call-done
  529.6 3.2 convert_select_fusion
  532.8 11.5 scatter_custom_fusion
  544.3 13.1 %scatter_fusion = f32[3584,192]{1,0:T(8,128)} fusion(f32[3584,192]{1,0:T(8,128)} %scatter_custom_fusion, s32[1536]{0:T(1024)S(1)} %get-tuple-element.185, f32[1536,192]{1,0:T(8,128)} %bitcast.204), kind=kCustom, calls=%fused_computation.5 | custom fusion | flops 294912 | bytes 3545088
  557.4 13.1 %scatter_fusion.1 = f32[3584,192]{1,0:T(8,128)} fusion(f32[3584,192]{1,0:T(8,128)} %scatter_fusion, s32[1536]{0:T(1024)S(1)} %get-tuple-element.184, f32[1536,192]{1,0:T(8,128)} %bitcast.206), kind=kCustom, calls=%fused_computation.6 | custom fusion | flops 294912 | bytes 3545088
  570.5 13.1 %scatter_fusion.2 = f32[3584,192]{1,0:T(8,128)} fusion(f32[3584,192]{1,0:T(8,128)} %scatter_fusion.1, s32[1536]{0:T(1024)S(1)} %get-tuple-element.183, f32[1536,192]{1,0:T(8,128)} %bitcast.205), kind=kCustom, calls=%fused_computation.7 | custom fusion | flops 294912 | bytes 3545088
  583.6 5.5 copy.185
  589.2 18.9 %reduce-scatter.17.cloned.1.call-done = f32[192,768]{1,0:T(8,128)} async-done(((f32[768,768]{1,0:T(8,128)}), f32[192,768]{1,0:T(8,128)}) %reduce-scatter.17.cloned.1.call-update) | async-done | bytes 589840 | tf_op jit(solution)/shard_map/reduce_scatter | solution.py:322
  608.1 115.0 %reduce-scatter.21.cloned.1.call-done = f32[512,768]{1,0:T(8,128)} async-done(((f32[2048,768]{1,0:T(8,128)}), f32[512,768]{1,0:T(8,128)}) %reduce-scatter.21.cloned.1.call-update) | async-done | bytes 1572880 | tf_op jit(solution)/shard_map/reduce_scatter | solution.py:324
  723.1 126.2 %reduce-scatter.15.cloned.1.call-done = f32[192,2304]{1,0:T(8,128)} async-done(((f32[768,2304]{1,0:T(8,128)}), f32[192,2304]{1,0:T(8,128)}) %reduce-scatter.15.cloned.1.call-update) | async-done | bytes 1769488 | tf_op jit(solution)/shard_map/reduce_scatter | solution.py:321
  849.3 214.7 %reduce-scatter.19.cloned.1.call-done = f32[192,4096]{1,0:T(8,128)} async-done(((f32[768,4096]{1,0:T(8,128)}), f32[192,4096]{1,0:T(8,128)}) %reduce-scatter.19.cloned.1.call-update) | async-done | bytes 3145744 | tf_op jit(solution)/shard_map/reduce_scatter | solution.py:323
  1064.1 3.9 fusion.31
  1072.2 11.5 reduce-scatter.25.cloned.1.call-done
  1084.6 13.5 %psum.55 = f32[2,192]{1,0:T(2,128)} all-reduce(f32[2,192]{1,0:T(2,128)S(1)} %copy.187), channel_id=1, replica_groups=mesh['fsdp'=4,'rep'=8] {'rep'}, use_global_device_ids=true, to_apply=%region_46.47 | all-reduce | flops 384 | bytes 3072 | tf_op jit(solution)/shard_map/psum | solution.py:329
  1098.2 141.7 %all-reduce.7.cloned.1.call-done = (f32[2,1792,192]{1,0,2:T(2,128)}, f32[192,2304]{1,0:T(8,128)}, f32[192,768]{1,0:T(8,128)}, f32[192,4096]{1,0:T(8,128)}, f32[512,768]{1,0:T(8,128)}, /*index=5*/f32[96,768]{1,0:T(8,128)}) async-done(((f32[2,1792,192]{1,0,2:T(2,128)}, f32[192,2304]{1,0:T(8,128)}, f32[192,768]{1,0:T(8,128)}, f32[192,4096]{1,0:T(8,128)}, f32[512,768]{1,0:T(8,128)}, ...) | async-done | bytes 10125328 | tf_op jit(solution)/shard_map/psum | solution.py:329
  1239.9 3.7 copy.176
  (381 shorter events, 110.2 us)
Async XLA Ops:
  7.2 71.8 %reduce-scatter.13.cloned.1.call-start = ((), (), s32[]{:S(2)}) async-start(), calls=%async_computation.13 | async-start | bytes 1474560 | tf_op jit(solution)/shard_map/reduce_scatter | solution.py:300
  25.9 5.3 copy-start.88
  33.0 71.4 %reduce-scatter.11.cloned.1.call-start = ((), (), s32[]{:S(2)}) async-start(), calls=%async_computation.8 | async-start | bytes 1474560 | tf_op jit(solution)/shard_map/reduce_scatter | solution.py:300
  44.8 129.6 %all-gather.10.cloned.1.call-start = ((), (), s32[]{:S(2)}) async-start(), calls=%async_computation.9 | async-start | bytes 4423680 | tf_op jit(solution)/shard_map/all_gather | solution.py:276
  45.5 161.0 %all-gather.12.cloned.1.call-start = ((), (), s32[]{:S(2)}) async-start(), calls=%async_computation.10 | async-start | bytes 1474560 | tf_op jit(solution)/shard_map/all_gather | solution.py:277
  46.1 23.7 %copy-start.97 = (bf16[2,192]{1,0:T(2,128)(2,1)S(1)}, bf16[2,192]{1,0:T(2,128)(2,1)}, u32[]{:S(2)}) copy-start(bf16[2,192]{1,0:T(2,128)(2,1)} %param.23) | copy-start | bytes 2308
  46.1 32.0 %copy-start.96 = (s32[2,1,384]{2,1,0:T(1,128)S(1)}, s32[2,1,384]{2,1,0:T(1,128)}, u32[]{:S(2)}) copy-start(s32[2,1,384]{2,1,0:T(1,128)} %param.16) | copy-start | bytes 9220
  46.1 32.8 %copy-start.60 = (bf16[2,1,384,768]{3,2,1,0:T(8,128)(2,1)S(1)}, bf16[2,1,384,768]{3,2,1,0:T(8,128)(2,1)}, u32[]{:S(2)}) copy-start(bf16[2,1,384,768]{3,2,1,0:T(8,128)(2,1)} %param.12) | copy-start | bytes 3538948
  46.1 274.3 %all-gather.14.cloned.1.call-start = ((), (), s32[]{:S(2)}) async-start(), calls=%async_computation.11 | async-start | bytes 7864320 | tf_op jit(solution)/shard_map/all_gather | solution.py:278
  46.7 337.3 %all-gather.16.cloned.1.call-start = ((), (), s32[]{:S(2)}) async-start(), calls=%async_computation.12 | async-start | bytes 3932160 | tf_op jit(solution)/shard_map/all_gather | solution.py:279
  47.3 466.9 %all-gather.18.cloned.1.call-start = ((), (), s32[]{:S(2)}) async-start(), calls=%async_computation.14 | async-start | bytes 1474560 | tf_op jit(solution)/shard_map/all_gather | solution.py:315
  69.8 34.7 %copy-start.11 = (bf16[384,768]{1,0:T(8,128)(2,1)}, bf16[384,768]{1,0:T(8,128)(2,1)S(1)}, u32[]{:S(2)}) copy-start(bf16[384,768]{1,0:T(8,128)(2,1)S(1)} %all_gather.28) | copy-start | bytes 1769476
  78.6 118.1 %copy-start.74 = (f32[384,32]{0,1:T(8,128)}, f32[384,32]{0,1:T(8,128)S(1)}, u32[]{:S(2)}) copy-start(f32[384,32]{0,1:T(8,128)S(1)} %get-tuple-element.155) | copy-start | bytes 147460
  78.6 130.1 %copy-start.76 = (f32[384,32]{0,1:T(8,128)}, f32[384,32]{0,1:T(8,128)S(1)}, u32[]{:S(2)}) copy-start(f32[384,32]{0,1:T(8,128)S(1)} %get-tuple-element.150) | copy-start | bytes 147460
  78.6 130.1 %copy-start.78 = (f32[384,32]{0,1:T(8,128)}, f32[384,32]{0,1:T(8,128)S(1)}, u32[]{:S(2)}) copy-start(f32[384,32]{0,1:T(8,128)S(1)} %get-tuple-element.151) | copy-start | bytes 147460
  106.1 73.5 %copy-start.13 = (f32[384,768]{1,0:T(8,128)}, f32[384,768]{1,0:T(8,128)S(1)}, u32[]{:S(2)}) copy-start(f32[384,768]{1,0:T(8,128)S(1)} %get-tuple-element.163) | copy-start | bytes 3538948
  204.0 4.7 copy-start.33
  217.2 195.8 %copy-start.80 = (f32[12,384]{1,0:T(8,128)}, f32[12,384]{1,0:T(8,128)S(1)}, u32[]{:S(2)}) copy-start(f32[12,384]{1,0:T(8,128)S(1)} %log_add_fusion.1) | copy-start | bytes 55300
  320.4 7.6 copy-start.2
  320.4 7.6 copy-start.3
  384.0 7.5 copy-start.21
  384.0 7.5 copy-start.25
  384.0 7.5 copy-start.102
  384.0 11.8 slice-start.4
  391.5 4.3 slice-start.5
  407.6 5.4 copy-start.42
  407.6 13.3 %slice-start.2 = ((s8[7077888]{0:T(1024)(128)(4,1)}), s8[4194304]{0:T(1024)(128)(4,1)S(1)}, s32[]{:S(2)}) async-start(s8[7077888]{0:T(1024)(128)(4,1)} %bitcast.199), calls=%async_computation.25 | async-start | bytes 8388608
  413.0 8.0 slice-start.3
  433.9 5.4 copy-start.38
  434.0 13.5 %slice-start = ((s8[7077888]{0:T(1024)(128)(4,1)}), s8[4194304]{0:T(1024)(128)(4,1)S(1)}, s32[]{:S(2)}) async-start(s8[7077888]{0:T(1024)(128)(4,1)} %bitcast.197), calls=%async_computation.23 | async-start | bytes 8388608
  439.4 8.1 slice-start.1
  455.8 4.5 copy-start.39
  455.9 4.4 copy-start.40
  460.8 4.7 copy-start.47
  460.9 4.6 copy-start.49
  467.5 62.1 %all-gather.20.cloned.1.call-start = ((), (), s32[]{:S(2)}) async-start(), calls=%async_computation.15 | async-start | bytes 1474560 | tf_op jit(solution)/shard_map/all_gather | solution.py:315
  471.8 117.4 %reduce-scatter.23.cloned.1.call-start = ((), (), s32[]{:S(2)}) async-start(), calls=%async_computation.20 | async-start | bytes 1474560 | tf_op jit(solution)/shard_map/reduce_scatter | solution.py:325
  475.1 133.0 %reduce-scatter.17.cloned.1.call-start = ((), (), s32[]{:S(2)}) async-start(), calls=%async_computation.17 | async-start | bytes 2949120 | tf_op jit(solution)/shard_map/reduce_scatter | solution.py:322
  479.8 243.3 %reduce-scatter.21.cloned.1.call-start = ((), (), s32[]{:S(2)}) async-start(), calls=%async_computation.19 | async-start | bytes 7864320 | tf_op jit(solution)/shard_map/reduce_scatter | solution.py:324
  488.2 361.2 %reduce-scatter.15.cloned.1.call-start = ((), (), s32[]{:S(2)}) async-start(), calls=%async_computation.16 | async-start | bytes 8847360 | tf_op jit(solution)/shard_map/reduce_scatter | solution.py:321
  498.2 565.8 %reduce-scatter.19.cloned.1.call-start = ((), (), s32[]{:S(2)}) async-start(), calls=%async_computation.18 | async-start | bytes 15728640 | tf_op jit(solution)/shard_map/reduce_scatter | solution.py:323
  499.5 5.6 copy-start.53
  499.5 5.6 copy-start.55
  512.0 571.7 %reduce-scatter.25.cloned.1.call-start = ((), (), s32[]{:S(2)}) async-start(), calls=%async_computation.21 | async-start | bytes 491520
  514.2 725.7 %all-reduce.7.cloned.1.call-start = ((), (), s32[]{:S(2)}) async-start(), calls=%async_computation.22 | async-start | bytes 20250624 | tf_op jit(solution)/shard_map/psum | solution.py:329
  514.3 15.3 %copy-start.87 = (pred[4,384]{1,0:T(4,128)(4,1)S(1)}, pred[4,384]{1,0:T(4,128)(4,1)}, u32[]{:S(2)}) copy-start(pred[4,384]{1,0:T(4,128)(4,1)} %copy-done.86) | copy-start | bytes 4612
  514.3 15.3 %copy-start.89 = (pred[4,384]{1,0:T(4,128)(4,1)S(1)}, pred[4,384]{1,0:T(4,128)(4,1)}, u32[]{:S(2)}) copy-start(pred[4,384]{1,0:T(4,128)(4,1)} %copy-done.88) | copy-start | bytes 4612
  1239.9 4.9 copy-start.73
  (77 other events, 167.9 us)
Sparse Core Ops, SparseCore 0:
  33.1 39.8 reduce-scatter.12
  75.9 28.4 reduce-scatter.10
  106.0 68.3 all-gather.9
  175.8 30.7 all-gather.11
  208.0 112.4 all-gather.13
  321.9 62.0 all-gather.15
  467.7 30.7 all-gather.17
  500.0 29.5 all-gather.19
  531.9 27.0 reduce-scatter.22
  561.7 46.3 reduce-scatter.16
  610.4 112.6 reduce-scatter.20
  725.3 124.0 reduce-scatter.14
  851.7 212.3 reduce-scatter.18
  1066.2 17.4 reduce-scatter.24
  1089.6 150.2 all-reduce.6
where the time goes:
time: 1270 us; the launch traced here: 1260 us
  waiting for transfers between devices  892 us (70%)
  matrix products  137 us (11%)
  other arithmetic  83.1 us (7%)
  local copies, waits for them, and re-layouts  75.8 us (6%)
  blocking collectives  53.2 us (4%)
  between operations  16 us (1%)
    reduce_scatter x1, waiting for transfers between devices, body(): lax.psum_scatter(gate_up_part, 'fsdp', scatter_dimension=0, tiled=True)  215 us
    psum x1, waiting for transfers between devices, body(): lax.psum((weight_totals[0], weight_totals[1], weight_totals[2], weight_to...  142 us
    reduce_scatter x1, waiting for transfers between devices, body(): lax.psum_scatter(qkv_part, 'fsdp', scatter_dimension=0, tiled=True)  126 us
    reduce_scatter x1, waiting for transfers between devices, body(): lax.psum_scatter(down_part, 'fsdp', scatter_dimension=0, tiled=True)  115 us
    all_gather x1, waiting for transfers between devices, body(): lax.all_gather(w_gate_up, 'fsdp', axis=0, tiled=True)  103 us
    all_gather x1, waiting for transfers between devices, body(): lax.all_gather(w_qkv, 'fsdp', axis=0, tiled=True)  68.2 us
    unnamed x13, other arithmetic  53.4 us
    all_gather x1, waiting for transfers between devices, body(): lax.all_gather(w_down, 'fsdp', axis=0, tiled=True)  51.4 us
  transfers between devices with their start and end apart: 15, of which 12 were waited for; matrix products, arithmetic and copies ran while one was open for 14% of the time, Pallas kernels for 0%

commit v1 on v0

v1 whole, which is shorter than its diff:
```python
import jax
import jax.numpy as jnp
import numpy as np
from jax import lax
from jax.experimental import pallas as pl
from jax.experimental.pallas import tpu as pltpu
from jax.sharding import Mesh, PartitionSpec as P

BF16 = jnp.bfloat16
F32 = jnp.float32
HEADS = 12
HEAD_DIM = 64
norm_eps = 1e-05
theta_base = 10000.0
masked_score = -1e30
MIB = 1 << 20

NN = (((1,), (0,)), ((), ()))
NT = (((1,), (1,)), ((), ()))
TN = (((0,), (0,)), ((), ()))


def mm(left, right, dims=NN):
    return lax.dot_general(left, right, dims, preferred_element_type=F32)


def full(shape):
    return pl.BlockSpec(shape, lambda *_: (0,) * len(shape))


def kernel_call(
    kernel, coords, args, in_specs, out_shape, out_specs, grid, scratch=(), flops=0, vmem=48, name=None
):
    moved = sum(a.size * a.dtype.itemsize for a in args)
    moved += sum(int(np.prod(s.shape)) * s.dtype.itemsize for s in out_shape)
    return pl.pallas_call(
        kernel,
        out_shape=out_shape,
        grid_spec=pltpu.PrefetchScalarGridSpec(
            num_scalar_prefetch=1,
            grid=grid,
            in_specs=in_specs,
            out_specs=out_specs,
            scratch_shapes=list(scratch),
        ),
        compiler_params=pltpu.CompilerParams(vmem_limit_bytes=vmem * MIB),
        cost_estimate=pl.CostEstimate(flops=int(flops), bytes_accessed=int(moved), transcendentals=0),
        name=name,
    )(coords, *args)


def by_core(value):
    return lax.ppermute(value, "oct", [(i, i ^ 1) for i in range(8)])


def by_x(value):
    return lax.ppermute(value, "oct", [(i, i ^ 2) for i in range(8)])


def by_y(value):
    return lax.ppermute(value, "oct", [(i, i ^ 4) for i in range(8)])


def from_ahead(value, step, size):
    return lax.ppermute(value, "fsdp", [((i + step) % size, i) for i in range(size)])


def to_ahead(value, step, size):
    return lax.ppermute(value, "fsdp", [(i, (i + step) % size) for i in range(size)])


def gather_plane(piece, depth, axis, cut):
    held = jnp.stack([from_ahead(piece, step, depth) for step in range(1, depth)])
    from_x = by_x(held)
    from_y = by_y(held)
    low = by_y(lax.slice_in_dim(from_x, 0, cut, axis=axis))
    high = by_x(lax.slice_in_dim(from_y, cut, held.shape[axis], axis=axis))
    return held, from_x, from_y, low, high


def add_low(left, right):
    return (left.astype(F32) + right.astype(F32)).astype(BF16)


def reduce_all(parts, depth):
    half = depth // 2
    kept = add_low(parts[0], by_core(parts[1]))
    a_part, b_part = kept[:, :half], kept[:, half:]
    a_part = add_low(a_part[0::2], by_x(a_part[1::2]))
    b_part = add_low(b_part[:2], by_y(b_part[2:]))
    a_part = add_low(a_part[0], by_y(a_part[1]))
    b_part = add_low(b_part[0], by_x(b_part[1]))
    return over_depth([a_part[i] for i in range(half)] + [b_part[i] for i in range(depth - half)], depth)


def over_depth(shards, depth):
    total = shards[0].astype(F32)
    for step in range(1, depth):
        total = total + to_ahead(shards[step], step, depth).astype(F32)
    return total


def over_groups(value, groups):
    if groups > 1:
        value = lax.psum(value, "grp")
    return value


def spread(value, octet, send_core=True):
    def pair(mine, other, bit):
        first = bit == 0
        return jnp.stack([jnp.where(first, mine, other), jnp.where(first, other, mine)])

    value = pair(value, by_x(value), (octet >> 1) & 1)
    value = pair(value, by_y(value), octet >> 2)
    value = pair(value, by_core(value), octet & 1)
    return value


def swap_halves(values):
    lane = lax.broadcasted_iota(jnp.int32, values.shape, 1)
    return jnp.where((lane & 63) < 32, pltpu.roll(values, 96, 1), pltpu.roll(values, 32, 1))


def project_kernel(
    coords, rows_own, rows_other, embedded, up_own, gain, qkv_own, out_own,
    a0, ax, ay, al, ah, c0, cx, cy, cl, ch,
    b0, bx, by, bl, bh, d0, dx, dy, dl, dh,
    cosine, sine,
    residual, queries, keys, values, w_qkv, w_out, w_up,
):
    depth_at, plane_at, core_at = coords[0], coords[1], coords[2]

    @pl.when(pl.program_id(0) == 0)
    def _():
        w_up[pl.ds(pl.multiple_of(depth_at * 96, 32), 96), :] = up_own[...]
        base = pl.multiple_of(depth_at * 192, 64)
        w_qkv[0, pl.ds(base, 192), :] = qkv_own[:, 0:1152]
        w_qkv[1, pl.ds(base, 192), :] = qkv_own[:, 1152:2304]
        w_out[pl.ds(base, 192), :] = out_own[...]
        groups = (
            (core_at, (a0, ax, ay, al, ah), (b0, bx, by, bl, bh)),
            (1 - core_at, (c0, cx, cy, cl, ch), (d0, dx, dy, dl, dh)),
        )
        for index, (core, tops, lows) in enumerate(groups):
            up_at = 224 if index == 0 else 0
            up_high = 96 if index == 0 else 0
            column = pl.multiple_of(core * 384, 128)
            for far in range(4):
                plane = plane_at ^ far
                for step in range(1, 4):
                    shard = (depth_at + step) % 4
                    row = pl.multiple_of(shard * 192 + plane * 48, 16)
                    at = step - 1
                    if far < 3:
                        block = lows[far][at]
                        w_qkv[core, pl.ds(row, 48), :] = block[:, 0:1152]
                        w_out[pl.ds(row, 48), pl.ds(column, 384)] = block[:, 1152:1536]
                    else:
                        w_qkv[core, pl.ds(row, 48), 0:768] = lows[3][at]
                        w_qkv[core, pl.ds(row, 48), 768:1152] = lows[4][at, :, 0:384]
                        w_out[pl.ds(row, 48), pl.ds(column, 384)] = lows[4][at, :, 384:768]

                    @pl.when(plane < 3)
                    def _():
                        up_row = pl.multiple_of(shard * 96 + plane * 32, 32)
                        if far < 3:
                            w_up[pl.ds(up_row, 32), pl.ds(column, 384)] = tops[far][at, up_at : up_at + 32, :]
                        else:
                            w_up[pl.ds(up_row, 32), pl.ds(column, 384)] = tops[4][at, up_high : up_high + 32, :]

    first = pl.multiple_of(core_at * 192, 64)
    second = pl.multiple_of(192 - core_at * 192, 64)
    total = embedded[...].astype(F32)
    total += mm(rows_own[...], w_up[pl.ds(first, 192), :])
    total += mm(rows_other[...], w_up[pl.ds(second, 192), :])
    residual[...] = total
    inverse = lax.rsqrt(jnp.mean(total * total, axis=-1, keepdims=True) + norm_eps)
    act = (total * inverse * gain[...]).astype(BF16)
    left = mm(act, w_qkv[0])
    right = mm(act, w_qkv[1])
    cos, sin = cosine[...], sine[...]
    for at in range(6):
        part = left[:, 128 * at : 128 * at + 128]
        turned = part * cos + swap_halves(part) * sin
        queries[:, 128 * at : 128 * at + 128] = (turned * 0.125).astype(BF16)
    for at in range(6):
        part = left[:, 768 + 128 * at : 896 + 128 * at] if at < 3 else right[:, 128 * at - 384 : 128 * at - 256]
        turned = part * cos + swap_halves(part) * sin
        keys[:, 128 * at : 128 * at + 128] = turned.astype(BF16)
    values[...] = right[:, 384:1152].astype(BF16)


def attend_kernel(
    coords, queries, keys, values, bias, residual, w_out, gain,
    attended, weights_out, middle, act_two, total,
):
    pair = pl.program_id(1)
    lane = lax.broadcasted_iota(jnp.int32, queries.shape, 1)
    q, k = queries[...], keys[...]
    v_t = jnp.transpose(values[...])
    outs = []
    for head in range(2):
        q_head = jnp.where((lane >= 64) == (head == 1), q, jnp.zeros_like(q))
        scores = mm(k, q_head, NT) + bias[0]
        top = jnp.max(scores, axis=0, keepdims=True)
        raised = jnp.exp(scores - top)
        weight = (raised * (1.0 / jnp.sum(raised, axis=0, keepdims=True))).astype(BF16)
        weights_out[0, 0, head] = weight
        outs.append(mm(v_t[64 * head : 64 * head + 64, :], weight))
    low = jnp.transpose(jnp.concatenate(outs, axis=0).astype(BF16))
    attended[...] = low
    part = mm(low, w_out[...])

    @pl.when(pair == 0)
    def _():
        total[...] = residual[...] + part

    @pl.when(pair > 0)
    def _():
        total[...] += part

    @pl.when(pair == 5)
    def _():
        mid = total[...]
        middle[...] = mid
        inverse = lax.rsqrt(jnp.mean(mid * mid, axis=-1, keepdims=True) + norm_eps)
        act_two[...] = (mid * inverse * gain[...]).astype(BF16)


def forward_kernel(
    coords, act, cotangent, middle, gain, w_gate, w_up, w_down,
    output, grads, grad_mid, grad_low, gain_grad, total, grad_act, act_t,
):
    at = pl.program_id(0)
    depth_at = coords[0]

    @pl.when(at == 0)
    def _():
        act_t[...] = jnp.transpose(act[...])

    a, c = act[...], cotangent[...]
    gate = mm(a, w_gate[...])
    up = mm(a, w_up[...])
    back = mm(c, w_down[...], NT)
    sig = 1.0 / (1.0 + jnp.exp(-gate))
    silu = gate * sig
    inner = (silu * up).astype(BF16)
    d_up = (back * silu).astype(BF16)
    d_gate = (back * up * (sig * (1.0 + gate * (1.0 - sig)))).astype(BF16)
    out_part = mm(inner, w_down[...])
    act_part = mm(d_gate, w_gate[...], NT) + mm(d_up, w_up[...], NT)

    @pl.when(at == 0)
    def _():
        total[...] = out_part
        grad_act[...] = act_part

    @pl.when(at > 0)
    def _():
        total[...] += out_part
        grad_act[...] += act_part

    down = mm(inner, c, TN).astype(BF16)
    gate_g = mm(act_t[...], d_gate).astype(BF16)
    up_g = mm(act_t[...], d_up).astype(BF16)
    for shard in range(4):
        far = (shard + 4 - depth_at) % 4
        grads[at, far, 0:192, :] = gate_g[192 * shard : 192 * shard + 192, :]
        grads[at + 4, far, 0:192, :] = up_g[192 * shard : 192 * shard + 192, :]
    far = (at + 4 - depth_at) % 4
    for q in range(8):
        grads[q, far, 192:256, :] = down[64 * q : 64 * q + 64, 0:512]
        grads[q, far, 256:288, 0:256] = down[64 * q : 64 * q + 32, 512:768]
        grads[q, far, 256:288, 256:512] = down[64 * q + 32 : 64 * q + 64, 512:768]

    @pl.when(at == 3)
    def _():
        mid = middle[...]
        output[...] = (mid + total[...]).astype(BF16)
        inverse = lax.rsqrt(jnp.mean(mid * mid, axis=-1, keepdims=True) + norm_eps)
        normed = mid * inverse
        grad = grad_act[...]
        gain_grad[...] = jnp.sum(grad * normed, axis=0, keepdims=True)
        n = grad * gain[...]
        g = c.astype(F32) + inverse * (n - normed * jnp.mean(n * normed, axis=-1, keepdims=True))
        grad_mid[...] = g
        grad_low[...] = g.astype(BF16)


def attend_back_kernel(
    coords, queries, keys, values, weights_in, grad_low, w_out, cosine, sine, grad_projected
):
    lane = lax.broadcasted_iota(jnp.int32, (384, 128), 1)
    grad_attended = mm(grad_low[...], w_out[...], NT).astype(BF16)
    for seq in range(2):
        rows = slice(384 * seq, 384 * seq + 384)
        q, k, v, ga = queries[rows, :], keys[rows, :], values[rows, :], grad_attended[rows, :]
        k_t = jnp.transpose(k)
        grad_k = jnp.zeros((384, 128), F32)
        grad_v = jnp.zeros((384, 128), F32)
        grad_q_t = []
        for head in range(2):
            mine = (lane >= 64) == (head == 1)
            ga_head = jnp.where(mine, ga, jnp.zeros_like(ga))
            q_head = jnp.where(mine, q, jnp.zeros_like(q))
            weight_low = weights_in[seq, 0, head]
            weight = weight_low.astype(F32)
            grad_weight = mm(v, ga_head, NT)
            row = jnp.sum(grad_weight * weight, axis=0, keepdims=True)
            grad_scores = (weight * (grad_weight - row)).astype(BF16)
            grad_v += mm(weight_low, ga_head)
            grad_k += mm(grad_scores, q_head)
            grad_q_t.append(mm(k_t[64 * head : 64 * head + 64, :], grad_scores))
        grad_q = jnp.transpose(jnp.concatenate(grad_q_t, axis=0)) * 0.125
        cos, sin = cosine[rows, :], sine[rows, :]
        grad_projected[0, rows, :] = (grad_q * cos - swap_halves(grad_q) * sin).astype(BF16)
        grad_projected[1, rows, :] = (grad_k * cos - swap_halves(grad_k) * sin).astype(BF16)
        grad_projected[2, rows, :] = grad_v.astype(BF16)


def embed_back_kernel(
    coords, grad_projected, w_qkv, w_up, residual, grad_mid, gain,
    embedding_grad, grad_rows, act, gain_grad,
):
    core_at = coords[2]
    dq, dk, dv = grad_projected[0], grad_projected[1], grad_projected[2]
    grad = mm(dq, w_qkv[0, :, 0:768], NT)
    grad += mm(dk[:, 0:384], w_qkv[0, :, 768:1152], NT)
    grad += mm(dk[:, 384:768], w_qkv[1, :, 0:384], NT)
    grad += mm(dv, w_qkv[1, :, 384:1152], NT)
    total = residual[...]
    inverse = lax.rsqrt(jnp.mean(total * total, axis=-1, keepdims=True) + norm_eps)
    normed = total * inverse
    act[...] = (normed * gain[...]).astype(BF16)
    part = jnp.sum(grad * normed, axis=0, keepdims=True)
    n = grad * gain[...]
    g = grad_mid[...] + inverse * (n - normed * jnp.mean(n * normed, axis=-1, keepdims=True))
    low = g.astype(BF16)
    embedding_grad[...] = low
    rows = mm(low, w_up[...], NT).astype(BF16)

    @pl.when(pl.program_id(0) == 0)
    def _():
        gain_grad[...] = part
        grad_rows[0, :, 0:192] = rows[:, 0:192]
        grad_rows[1, :, 0:192] = rows[:, 192:384]

    @pl.when(pl.program_id(0) == 1)
    def _():
        gain_grad[...] += part
        grad_rows[0, :, 192:384] = rows[:, 0:192]
        grad_rows[1, :, 192:384] = rows[:, 192:384]


def weight_grad_kernel(
    coords, act, grad_projected, attended, grad_low, rows_own, rows_other, embedding_grad, gains,
    grads, act_t, attended_t,
):
    depth_at, plane_at, core_at = coords[0], coords[1], coords[2]
    at = pl.program_id(0)

    @pl.when(at == 0)
    def _():
        act_t[...] = jnp.transpose(act[...])
        attended_t[...] = jnp.transpose(attended[...])

    def place(core, column, block):
        for plane in range(4):
            for shard in range(4):
                row = 192 * shard + 48 * plane
                grads[core ^ core_at, plane ^ plane_at, (shard + 4 - depth_at) % 4, 0:48, column] = block[
                    row : row + 48, :
                ]

    for step in range(6):
        @pl.when(at == step)
        def _():
            block = mm(act_t[...], grad_projected[0]).astype(BF16)
            start = 384 * (step % 3)
            place(step // 3, slice(start, start + 384), block)

    for step in range(2):
        @pl.when(at == 6 + step)
        def _():
            block = mm(attended_t[...], grad_low[:, 384 * step : 384 * step + 384]).astype(BF16)
            place(step, slice(1152, 1536), block)

    @pl.when(at == 8)
    def _():
        low = embedding_grad[...]
        mine = mm(rows_own[...], low, TN)
        other = mm(rows_other[...], low, TN)
        first = jnp.where(core_at == 0, mine, other)
        second = jnp.where(core_at == 0, other, mine)
        both = jnp.concatenate([first, second], axis=0)
        ones = gains[...]
        for core in range(2):
            for plane in range(4):
                for shard in range(4):
                    row = 96 * shard + 24 * plane
                    block = both[row : row + 24, 384 * core : 384 * core + 384]
                    extra = jnp.zeros((8, 384), F32)
                    if core == 0 and plane == 0:
                        line = jnp.concatenate(
                            [ones[0:1, 192 * shard : 192 * shard + 192], ones[1:2, 192 * shard : 192 * shard + 192]],
                            axis=1,
                        )
                        extra = jnp.concatenate([line, jnp.zeros((7, 384), F32)], axis=0)
                    block = jnp.concatenate([block, extra], axis=0).astype(BF16)
                    place_at = (core ^ core_at, plane ^ plane_at, (shard + 4 - depth_at) % 4)
                    grads[place_at[0], place_at[1], place_at[2], 48:64, 0:384] = block[0:16]
                    grads[place_at[0], place_at[1], place_at[2], 48:64, 384:768] = block[16:32]
                    grads[place_at[0], place_at[1], place_at[2], 48:64, 768:1536] = jnp.zeros((16, 768), BF16)


def table_kernel(coords, ids, own, from_x, from_y, low, high, sums, total):
    at = pl.program_id(0)

    def add(pairs):
        rows = jnp.concatenate([pairs[:, 0:192], pairs[:, 192:384]], axis=0)
        line = lax.broadcasted_iota(jnp.int32, (1792, 768), 0)
        hot = jnp.where(line == ids[0], 1.0, 0.0).astype(BF16)
        part = mm(hot, rows)

        @pl.when(at == 0)
        def _():
            total[...] = part

        @pl.when(at > 0)
        def _():
            total[...] += part

    for plane, source in enumerate((own, from_x, from_y)):
        for core in range(2):
            @pl.when(at == 2 * plane + core)
            def _():
                add(source[core])

    @pl.when(at == 6)
    def _():
        add(low[...].reshape(384, 384))

    @pl.when(at == 7)
    def _():
        add(high[...].reshape(384, 384))
        for shard in range(4):
            sums[shard, :, 0:192] = total[448 * shard : 448 * shard + 224, :].astype(BF16)
            sums[shard, :, 192:384] = total[448 * shard + 224 : 448 * shard + 448, :].astype(BF16)


def rotary_lanes(segments):
    seq_len = segments.shape[-1]
    position = jnp.arange(seq_len, dtype=jnp.int32)
    same = segments[:, :, None] == segments[:, None, :]
    start = jnp.min(jnp.where(same, position[None, None, :], seq_len), axis=-1)
    offset = (position[None, :] - start).astype(F32)
    half = HEAD_DIM // 2
    frequency = theta_base ** (-jnp.arange(half, dtype=F32) / half)
    angle = offset[..., None] * frequency
    cos, sin = jnp.cos(angle), jnp.sin(angle)
    cosine = jnp.concatenate([cos, cos, cos, cos], axis=-1)
    sine = jnp.concatenate([-sin, sin, -sin, sin], axis=-1)
    return cosine.reshape(-1, 128), sine.reshape(-1, 128), same


def sds(shape, dtype):
    return jax.ShapeDtypeStruct(shape, dtype)


def body(sizes, embedded, cotangent, ngram_ids, segments, live_mask, tables, w_qkv, w_out, w_gate_up, w_down, up_proj, norm_gains):
    depth, groups = sizes
    micro, _, seq, width = embedded.shape
    tokens = micro * seq
    rows_dev = tables.shape[1]
    depth_at = lax.axis_index("fsdp")
    octet = lax.axis_index("oct")
    core_at = octet & 1
    plane_at = octet >> 1
    coords = jnp.stack([depth_at, plane_at, core_at]).astype(jnp.int32)
    embedded = embedded.reshape(tokens, width)
    cotangent = cotangent.reshape(tokens, width)
    segments = segments.reshape(micro, seq)
    live_mask = live_mask.reshape(micro, seq)
    ids = ngram_ids.reshape(2, tokens)

    gate_rows = w_gate_up.shape[0] // 8
    down_rows = w_down.shape[0] // 8
    ff_gate_up = lax.all_gather(
        lax.dynamic_slice_in_dim(w_gate_up, octet * gate_rows, gate_rows, axis=0), ("fsdp", "oct"), axis=0, tiled=True
    )
    ff_down = lax.all_gather(
        lax.dynamic_slice_in_dim(w_down, octet * down_rows, down_rows, axis=0), ("fsdp", "oct"), axis=0, tiled=True
    )

    share = rows_dev // 4
    pairs = share // 2
    own_table = lax.dynamic_index_in_dim(tables, core_at, axis=0, keepdims=False).reshape(4, 2, pairs, 192)
    own_pairs = jnp.concatenate([own_table[:, 0], own_table[:, 1]], axis=-1)
    top = jnp.concatenate(
        [
            lax.dynamic_index_in_dim(own_pairs, plane_at, axis=0, keepdims=False),
            lax.dynamic_slice(up_proj, (jnp.minimum(plane_at, 2) * 32, core_at * 384), (32, 384)),
            jnp.pad(norm_gains, ((0, 6), (0, 192))),
        ],
        axis=0,
    )
    low = jnp.concatenate(
        [
            lax.dynamic_slice(w_qkv, (plane_at * 48, core_at * 1152), (48, 1152)),
            lax.dynamic_slice(w_out, (plane_at * 48, core_at * 384), (48, 384)),
        ],
        axis=1,
    )
    tops = gather_plane(top, depth, 1, 128)
    lows = gather_plane(low, depth, 2, 768)
    tops_other = [by_core(piece[:, 224:256] if i < 3 else (piece[:, 0:8] if i == 3 else piece[:, 96:128])) for i, piece in enumerate(tops)]
    lows_other = [by_core(piece) for piece in lows]

    gains_rel = jnp.concatenate([norm_gains[None], tops[0][:, 256:258, 0:192]], axis=0)
    gains = jnp.roll(gains_rel, depth_at, axis=0).transpose(1, 0, 2).reshape(2, width).astype(F32)
    gain_one, gain_two = gains[0:1], gains[1:2]

    ids_other = by_core(ids)
    wanted = jnp.stack(
        [
            lax.dynamic_index_in_dim(ids, core_at, axis=0, keepdims=False),
            lax.dynamic_index_in_dim(ids_other, core_at, axis=0, keepdims=False),
        ]
    )
    shard = wanted // rows_dev
    inside = wanted - shard * rows_dev
    plane = inside // share
    line = inside - plane * share
    in_second = line >= pairs
    line_pair = jnp.where(in_second, line - pairs, line)
    step = (shard - depth_at) % depth
    flat = jnp.where(
        step == 0,
        plane * pairs + line_pair,
        4 * pairs + ((plane ^ plane_at) * (depth - 1) + step - 1) * pairs + line_pair,
    )
    diagonal = jnp.concatenate([tops[3], tops[4][:, : pairs - 128]], axis=1)
    lookup = jnp.concatenate(
        [own_pairs.reshape(-1, 384)]
        + [piece[:, :pairs].reshape(-1, 384) for piece in (tops[0], tops[1], tops[2], diagonal)],
        axis=0,
    )
    picked = lookup.at[flat.reshape(-1)].get(mode="promise_in_bounds").reshape(2, tokens, 384)
    picked = jnp.where(in_second[..., None], picked[..., 192:], picked[..., :192])
    rows_own = picked[0]
    rows_other = by_core(picked[1])

    ids_x = by_x(wanted)
    near = jnp.stack([wanted, ids_x])
    plane_ids = jnp.concatenate([near, by_y(near)], axis=0)
    t_shard = plane_ids // rows_dev
    t_inside = plane_ids - t_shard * rows_dev
    t_plane = t_inside // share
    target = jnp.where(
        t_plane == plane_at, ((t_shard - depth_at) % depth) * share + t_inside - t_plane * share, -1
    ).reshape(8, 1, tokens)

    cosine, sine, same = rotary_lanes(segments)
    position = jnp.arange(seq, dtype=jnp.int32)
    usable = same & (position[None, :, None] <= position[None, None, :]) & (live_mask[:, :, None] == 1)
    usable = usable | (position[None, :, None] == position[None, None, :])
    bias = jnp.where(usable, 0.0, masked_score).astype(F32)

    block = lambda w: pl.BlockSpec((seq, w), lambda i, *_: (i, 0))
    top_specs = [full(piece.shape) for piece in tops]
    low_specs = [full(piece.shape) for piece in lows]
    residual, queries, keys, values, qkv_full, out_full, up_full = kernel_call(
        project_kernel,
        coords,
        [rows_own, rows_other, embedded, up_proj, gain_one, w_qkv, w_out]
        + [p[:, :256] if i < 3 else p for i, p in enumerate(tops)]
        + [t if i in (3,) else t for i, t in enumerate(tops_other)]
        + list(lows) + list(lows_other) + [cosine, sine],
        [block(192), block(192), block(width), full(up_proj.shape), full((1, width)), full(w_qkv.shape), full(w_out.shape)]
        + [full((depth - 1, 256, 384)) if i < 3 else s for i, s in enumerate(top_specs)]
        + [full(t.shape) for t in tops_other] + low_specs + low_specs + [block(128), block(128)],
        [sds((tokens, width), F32)] + [sds((tokens, width), BF16)] * 3
        + [sds((2, width, 1152), BF16), sds((width, width), BF16), sds((384, width), BF16)],
        [block(width)] * 4 + [full((2, width, 1152)), full((width, width)), full((384, width))],
        (micro,),
        flops=2 * tokens * width * 2688,
        vmem=56,
        name="project",
    )

    pair_block = pl.BlockSpec((seq, 128), lambda s, p, *_: (s, p))
    seq_block = pl.BlockSpec((seq, width), lambda s, p, *_: (s, 0))
    attended, weights, middle, act_two = kernel_call(
        attend_kernel,
        coords,
        [queries, keys, values, bias, residual, out_full, gain_two],
        [pair_block, pair_block, pair_block, pl.BlockSpec((1, seq, seq), lambda s, p, *_: (s, 0, 0)), seq_block,
         pl.BlockSpec((128, width), lambda s, p, *_: (p, 0)), full((1, width))],
        [sds((tokens, width), BF16), sds((micro, 6, 2, seq, seq), BF16), sds((tokens, width), F32), sds((tokens, width), BF16)],
        [pair_block, pl.BlockSpec((1, 1, 2, seq, seq), lambda s, p, *_: (s, p, 0, 0, 0)), seq_block, seq_block],
        (micro, 6),
        scratch=[pltpu.VMEM((seq, width), F32)],
        flops=4 * tokens * seq * width + 2 * tokens * width * width,
        name="attend",
    )

    whole = full((tokens, width))
    output, ff_grads, grad_mid, grad_low, gain_two_grad = kernel_call(
        forward_kernel,
        coords,
        [act_two, cotangent, middle, gain_two, ff_gate_up, ff_gate_up, ff_down],
        [whole, whole, whole, full((1, width)),
         pl.BlockSpec((width, 512), lambda i, *_: (0, i)), pl.BlockSpec((width, 512), lambda i, *_: (0, i + 4)),
         pl.BlockSpec((512, width), lambda i, *_: (i, 0))],
        [sds((tokens, width), BF16), sds((8, 4, 288, 512), BF16), sds((tokens, width), F32), sds((tokens, width), BF16), sds((1, width), F32)],
        [whole, full((8, 4, 288, 512)), whole, whole, full((1, width))],
        (4,),
        scratch=[pltpu.VMEM((tokens, width), F32), pltpu.VMEM((tokens, width), F32), pltpu.VMEM((width, tokens), BF16)],
        flops=18 * tokens * width * 2048,
        vmem=60,
        name="feed",
    )
    ff_part = lax.psum_scatter(ff_grads, "oct", scatter_dimension=0, tiled=True)[0]

    back_block = pl.BlockSpec((tokens, 128), lambda p, *_: (0, p))
    (grad_projected,) = kernel_call(
        attend_back_kernel,
        coords,
        [queries, keys, values, weights, grad_low, out_full, cosine, sine],
        [back_block, back_block, back_block, pl.BlockSpec((micro, 1, 2, seq, seq), lambda p, *_: (0, p, 0, 0, 0)),
         whole, pl.BlockSpec((128, width), lambda p, *_: (p, 0)), full((tokens, 128)), full((tokens, 128))],
        [sds((3, tokens, width), BF16)],
        [pl.BlockSpec((3, tokens, 128), lambda p, *_: (0, 0, p))],
        (6,),
        flops=8 * tokens * seq * width + 2 * tokens * width * width,
        name="attend_back",
    )

    embedding_grad, grad_rows, act_one, gain_one_grad = kernel_call(
        embed_back_kernel,
        coords,
        [grad_projected, qkv_full, up_full, residual, grad_mid, gain_one],
        [pl.BlockSpec((3, seq, width), lambda i, *_: (0, i, 0)), full((2, width, 1152)), full((384, width)),
         block(width), block(width), full((1, width))],
        [sds((tokens, width), BF16), sds((2, seq, 384), BF16), sds((tokens, width), BF16), sds((1, width), F32)],
        [block(width), full((2, seq, 384)), block(width), full((1, width))],
        (micro,),
        flops=2 * tokens * width * 2688,
        name="embed_back",
    )

    mine = lax.dynamic_index_in_dim(grad_rows, core_at, axis=0, keepdims=False)
    other = by_core(lax.dynamic_index_in_dim(grad_rows, 1 - core_at, axis=0, keepdims=False))
    held = jnp.stack([mine, other])
    held_x, held_y = by_x(held), by_y(held)
    held_low, held_high = by_y(held_x[0]), by_x(held_y[1])

    gain_grads = jnp.concatenate([gain_one_grad, gain_two_grad], axis=0)
    (grads,) = kernel_call(
        weight_grad_kernel,
        coords,
        [act_one, grad_projected, attended, grad_low, rows_own, rows_other, embedding_grad, gain_grads],
        [whole, pl.BlockSpec((1, tokens, 384), lambda i, *_: (jnp.minimum(i, 5) // 2, 0, jnp.minimum(i, 5) % 2)), whole, whole,
         full((tokens, 192)), full((tokens, 192)), whole, full((2, width))],
        [sds((2, 4, 4, 64, 1536), BF16)],
        [full((2, 4, 4, 64, 1536))],
        (9,),
        scratch=[pltpu.VMEM((width, tokens), BF16), pltpu.VMEM((width, tokens), BF16)],
        flops=2 * tokens * width * 3456,
        name="weight_grad",
    )
    (table_sums,) = kernel_call(
        table_kernel,
        coords,
        [target, held, held_x, held_y, held_low, held_high],
        [pl.BlockSpec((1, 1, tokens), lambda i, *_: (i, 0, 0))] + [full((2, seq, 384))] * 3 + [full((seq, 384))] * 2,
        [sds((4, pairs, 384), BF16)],
        [full((4, pairs, 384))],
        (8,),
        scratch=[pltpu.VMEM((4 * share, 192), F32)],
        flops=2 * 8 * tokens * 4 * share * 192,
        name="table_sum",
    )

    weights_sum = reduce_all(grads, depth)
    table_sum = over_depth([table_sums[i] for i in range(depth)], depth)
    ff_sum = over_depth([ff_part[i] for i in range(depth)], depth)
    weights_sum, table_sum, ff_sum = (over_groups(v, groups).astype(BF16) for v in (weights_sum, table_sum, ff_sum))

    table_all = spread(table_sum, octet)
    weights_all = spread(weights_sum, octet)
    ff_all = lax.all_gather(ff_sum, "oct", axis=0)

    table_all = table_all.reshape(2, 4, pairs, 2, 192).transpose(0, 1, 3, 2, 4)
    table_grad = table_all.reshape(2, rows_dev, 192).astype(F32)
    tail = weights_all.reshape(2, 4, 64, 1536).astype(F32)
    qkv_grad = tail[:, :, 0:48, 0:1152].transpose(1, 2, 0, 3).reshape(192, 2304)
    out_grad = tail[:, :, 0:48, 1152:1536].transpose(1, 2, 0, 3).reshape(192, 768)
    up_all = jnp.concatenate([tail[:, :, 48:64, 0:384], tail[:, :, 48:64, 384:768]], axis=2)
    up_grad = up_all[:, :, 0:24].transpose(1, 2, 0, 3).reshape(96, 768)
    gains_grad = up_all[0, 0, 24].reshape(2, 192)
    ff_all = ff_all.astype(F32)
    gate_up_grad = ff_all[:, 0:192].transpose(1, 0, 2).reshape(192, 4096)
    down_right = jnp.concatenate([ff_all[:, 256:288, 0:256], ff_all[:, 256:288, 256:512]], axis=1)
    down_grad = jnp.concatenate([ff_all[:, 192:256], down_right], axis=2).reshape(512, 768)
    return (
        output.reshape(micro, 1, seq, width),
        embedding_grad.reshape(micro, 1, seq, width),
        table_grad,
        qkv_grad,
        out_grad,
        gate_up_grad,
        down_grad,
        up_grad,
        gains_grad,
    )


def solution(mesh):
    depth, rep = mesh.devices.shape
    groups = rep // 8
    fine = Mesh(mesh.devices.reshape(depth, groups, 8), ("fsdp", "grp", "oct"))
    every = ("fsdp", "grp", "oct")
    in_specs = (
        P(None, every, None, None),
        P(None, every, None, None),
        P(None, None, every, None),
        P(None, every, None),
        P(None, every, None),
        P(None, "fsdp", None),
        P("fsdp", None),
        P("fsdp", None),
        P("fsdp", None),
        P("fsdp", None),
        P("fsdp", None),
        P(None, "fsdp"),
    )
    out_specs = (
        P(None, every, None, None),
        P(None, every, None, None),
        P(None, "fsdp", None),
        P("fsdp", None),
        P("fsdp", None),
        P("fsdp", None),
        P("fsdp", None),
        P("fsdp", None),
        P(None, "fsdp"),
    )

    def step(*args):
        return body((depth, groups), *args)

    return jax.shard_map(step, mesh=fine, in_specs=in_specs, out_specs=out_specs, check_vma=False)
```

time: 1270 us -> 466 us (0.37)
  waiting for transfers between devices: 892 us -> 153 us
  matrix products: 137 us -> 0 us
  Pallas kernels: 0 us -> 129 us
  starting transfers between devices: 0.99 us -> 62.5 us
  blocking collectives: 53.2 us -> 0 us
  other arithmetic: 83.1 us -> 32 us
    reduce_scatter x7 -> x1, waiting for transfers between devices: 499 us -> 0.01 us  [body(): lax.psum_scatter(ff_grads, 'oct', scatter_dimension=0, tiled=True)[0]]
    all_gather x6 -> x3, waiting for transfers between devices: 238 us -> 15.2 us  [the longest x1 15.2 us: body(): lax.all_gather(lax.dynamic_slice_in_dim(w_gate_up, octet * gate_rows, gat...]
    psum x1 -> x0, waiting for transfers between devices: 142 us -> none  [body(): lax.psum((weight_totals[0], weight_totals[1], weight_totals[2], weight_to...]
    ppermute x0 -> x53, waiting for transfers between devices: none -> 138 us  [the longest x9 45.4 us: to_ahead(): lax.ppermute(value, 'fsdp', [(i, (i + step) % size) for i in range(size)])]
    dot_general x42 -> x0, matrix products: 137 us -> none  [the longest x2 16 us: backward_sequence(): jnp.einsum('qhd,khd->hqk', grad_attended, values, preferred_element_type=...]
    pallas_call x0 -> x7, Pallas kernels: none -> 129 us  [kernel_call(): pl.pallas_call(kernel, out_shape=out_shape, grid_spec=pltpu.PrefetchScala...]
    ppermute x0 -> x53, starting transfers between devices: none -> 62.3 us  [the longest x16 29.7 us: by_core(): return lax.ppermute(value, 'oct', [(i, i ^ 1) for i in range(8)])]
    unnamed x13 -> x3, other arithmetic: 53.4 us -> 1.31 us
  transfers between devices with their start and end apart: 15 -> 57, of which waited for: 12 -> 22; matrix products, arithmetic and copies ran while one was open for 14% -> 17% of each run, Pallas kernels for 0% -> 20%
where the time goes in v1:
time: 466 us; the launch traced here: 459 us
  waiting for transfers between devices  153 us (33%)
  Pallas kernels  129 us (28%)
  local copies, waits for them, and re-layouts  67.1 us (14%)
  starting transfers between devices  62.5 us (13%)
  other arithmetic  32 us (7%)
  between operations  15 us (3%)
    pallas_call x7, Pallas kernels, kernel_call(): pl.pallas_call(kernel, out_shape=out_shape, grid_spec=pltpu.PrefetchScala...  129 us
    ppermute x9, waiting for transfers between devices, to_ahead(): lax.ppermute(value, 'fsdp', [(i, (i + step) % size) for i in range(size)])  45.4 us
    ppermute x11, waiting for transfers between devices, by_x(): return lax.ppermute(value, 'oct', [(i, i ^ 2) for i in range(8)])  38.6 us
    ppermute x11, waiting for transfers between devices, by_y(): return lax.ppermute(value, 'oct', [(i, i ^ 4) for i in range(8)])  38.2 us
    ppermute x16, starting transfers between devices, by_core(): return lax.ppermute(value, 'oct', [(i, i ^ 1) for i in range(8)])  29.7 us
    unnamed x111, local copies, waits for them, and re-layouts  17.8 us
    all_gather x1, waiting for transfers between devices, body(): lax.all_gather(lax.dynamic_slice_in_dim(w_gate_up, octet * gate_rows, gat...  15.2 us
    ppermute x9, starting transfers between devices, to_ahead(): lax.ppermute(value, 'fsdp', [(i, (i + step) % size) for i in range(size)])  10.7 us
  transfers between devices with their start and end apart: 57, of which 22 were waited for; matrix products, arithmetic and copies ran while one was open for 17% of the time, Pallas kernels for 20%

profile of v1, /device:TPU:13, one launch (start us, length us, event | category | flops | bytes accessed | tf_op | source)
XLA Modules:
  0.0 459.0 jit_solution(15183381334234159511)
XLA Ops:
  7.2 1.7 constant_dynamic-slice_fusion.1
  16.7 2.3 collective-permute-start.2
  24.0 1.9 copy.69
  32.1 1.9 collective-permute-start.15
  34.7 7.3 %collective-permute-done.2 = bf16[264,384]{1,0:T(8,128)(2,1)} collective-permute-done((bf16[264,384]{1,0:T(8,128)(2,1)}, bf16[264,384]{1,0:T(8,128)(2,1)}, u32[]{:S(2)}, u32[]{:S(2)}) %collective-permute-start.2) | collective-permute-done | bytes 202784 | tf_op jit(solution)/shard_map/ppermute | solution.py:65
  45.4 2.6 collective-permute-done.14
  48.4 1.8 pad_maximum_fusion.5.b0
  51.8 3.5 collective-permute-start.21
  55.4 1.8 collective-permute-done.5
  60.6 7.5 %collective-permute-done.17.bx = bf16[3,48,1536]{2,1,0:T(8,128)(2,1)} collective-permute-done((bf16[3,48,1536]{2,1,0:T(8,128)(2,1)}, bf16[3,48,1536]{2,1,0:T(8,128)(2,1)}, u32[]{:S(2)}, u32[]{:S(2)}) %collective-permute-start.17) | collective-permute-done | bytes 442400 | tf_op jit(solution)/shard_map/ppermute | solution.py:57
  68.1 12.4 %collective-permute-start.9 = (bf16[3,32,384]{2,1,0:T(8,128)(2,1)}, bf16[3,32,384]{2,1,0:T(8,128)(2,1)}, u32[]{:S(2)}, u32[]{:S(2)}) collective-permute-start(bf16[3,32,384]{2,1,0:T(8,128)(2,1)} %slice.275), channel_id=1, source_target_pairs={{0,1},{1,0},{2,3},{3,2},{4,5},{5,4},{6,7},{7,6},{8,9},{9,8},{10,11... | collective-permute-start | bytes 221192 | tf_op jit(solution)/shard_map/ppermute | solution.py:53
  82.2 1.8 collective-permute-start.19
  87.5 5.3 %gather_fusion = bf16[1536,384]{1,0:T(8,128)(2,1)} fusion(bf16[3584,384]{1,0:T(8,128)(2,1)S(1)} %constant_dynamic-update-slice_fusion, s32[2048]{0:T(1024)S(1)} %pad_clamp_fusion), kind=kCustom, calls=%fused_computation | custom fusion | bytes 2365440 | tf_op jit(solution)/shard_map/gather | solution.py:549
  92.8 1.8 slice_select_fusion
  104.5 11.7 %project.1 = (f32[768,768]{1,0:T(8,128)}, bf16[768,768]{1,0:T(8,128)(2,1)}, bf16[768,768]{1,0:T(8,128)(2,1)}, bf16[768,768]{1,0:T(8,128)(2,1)}, bf16[2,768,1152]...) custom-call(s32[3]{0:T(128)} %pad_add_fusion.3.coords, ...), custom_call_target="tpu_custom_call" | custom-call | flops 3170893824 | bytes 21322752 | tf_op jit(solution)/shard_map/project/pallas_call | solution.py:36
  120.2 23.0 %attend.1 = (bf16[768,768]{1,0:T(8,128)(2,1)S(1)}, bf16[2,6,2,384,384]{4,3,2,1,0:T(8,128)(2,1)}, f32[768,768]{1,0:T(8,128)}, bf16[768,768]{1,0:T(8,128)(2,1)S(1)}) custom-call(s32[3]{0:T(128)S(1)} %copy-done.20, bf16[768,768]{1,0:T(8,128)(2,1)S(1)} %copy-done.3, bf16[768,768]{1,0:T(8,128)(2,1)S(1)} %copy-done.5, bf16[768,768]{1,0:T(8,128)(2,1)S(1)} %copy-done.7, ...), custom_call_target="tpu_custom_call" | custom-call | flops 1811939328 | bytes 20057088 | tf_op jit(solution)/shard_map/attend/pallas_call | solution.py:36
  145.3 15.2 %all-gather.5.cloned.1.call-done.w_gate.w_up = bf16[768,4096]{1,0:T(8,128)(2,1)} async-done(((bf16[24,4096]{1,0:T(8,128)(2,1)}), bf16[768,4096]{1,0:T(8,128)(2,1)}) %all-gather.5.cloned.1.call-update) | async-done | bytes 6291472 | tf_op jit(solution)/shard_map/all_gather | solution.py:489
  160.4 38.8 %feed.1 = (bf16[768,768]{1,0:T(8,128)(2,1)}, bf16[8,4,288,512]{3,2,1,0:T(8,128)(2,1)}, f32[768,768]{1,0:T(8,128)}, bf16[768,768]{1,0:T(8,128)(2,1)}, f32[1,768]{1,0:T(1,128)}) custom-call(s32[3]{0:T(128)} %pad_add_fusion.3.coords, bf16[768,768]{1,0:T(8,128)(2,1)} %copy-done.24, bf16[768,768]{1,0:T(8,128)(2,1)} %bitcast.208, ...), custom_call_target="tpu_custom_call" | custom-call | flops 21743271936 | bytes 34609152 | tf_op jit(solution)/shard_map/feed/pallas_call | solution.py:36
  204.6 22.1 %attend_back.1.grad_projected = bf16[3,768,768]{2,1,0:T(8,128)(2,1)} custom-call(s32[3]{0:T(128)S(1)} %copy-done.21, bf16[768,768]{1,0:T(8,128)(2,1)S(1)} %copy-done.4, bf16[768,768]{1,0:T(8,128)(2,1)S(1)} %copy-done.6, bf16[768,768]{1,0:T(8,128)(2,1)S(1)} %copy-done.8, bf16[2,6,2,384,384]{4,3,2,1,0:T(8,128)(2,1)} %get-tuple-element.37.weights_in, ...), custom_call_target="tpu_custom_call" | custom-call | flops 2717908992 | bytes 17301504 | tf_op jit(solution)/shard_map/attend_back/pallas_call | solution.py:36
  226.7 11.1 %embed_back.1 = (bf16[768,768]{1,0:T(8,128)(2,1)}, bf16[2,384,384]{2,1,0:T(8,128)(2,1)S(1)}, bf16[768,768]{1,0:T(8,128)(2,1)S(1)}, f32[1,768]{1,0:T(1,128)S(1)}) custom-call(s32[3]{0:T(128)S(1)} %copy-done.21, bf16[3,768,768]{2,1,0:T(8,128)(2,1)} %attend_back.1.grad_projected, bf16[2,768,1152]{2,1,0:T(8,128)(2,1)} %get-tuple-element.39.w_qkv, ...), custom_call_target="tpu_custom_call" | custom-call | flops 3170893824 | bytes 15341568 | tf_op jit(solution)/shard_map/embed_back/pallas_call | solution.py:36
  239.2 12.4 %weight_grad.1 = bf16[2,4,4,64,1536]{4,3,2,1,0:T(8,128)(2,1)} custom-call(s32[3]{0:T(128)S(1)} %copy-done.21, bf16[768,768]{1,0:T(8,128)(2,1)S(1)} %get-tuple-element.44.act, bf16[3,768,768]{2,1,0:T(8,128)(2,1)} %attend_back.1.grad_projected, bf16[768,768]{1,0:T(8,128)(2,1)S(1)} %copy-done.16, bf16[768,768]{1,0:T(8,128)(2,1)S(1)} %copy-done.10, ...), custom_call_target="tpu_custom_call" | custom-call | flops 4076863488 | bytes 15144960 | tf_op jit(solution)/shard_map/weight_grad/pallas_call | solution.py:36
  251.6 3.9 slice_bitcast_fusion.1
  256.1 5.4 %collective-permute-done.28 = bf16[384,384]{1,0:T(8,128)(2,1)S(1)} collective-permute-done((bf16[384,384]{1,0:T(8,128)(2,1)S(1)}, bf16[384,384]{1,0:T(8,128)(2,1)S(1)}, u32[]{:S(2)}, u32[]{:S(2)}) %collective-permute-start.28) | collective-permute-done | bytes 294944 | tf_op jit(solution)/shard_map/ppermute | solution.py:53
  263.6 21.7 %collective-permute-done.26 = s32[2,768]{1,0:T(2,128)S(1)} collective-permute-done((s32[2,768]{1,0:T(2,128)S(1)}, s32[2,768]{1,0:T(2,128)S(1)}, u32[]{:S(2)}, u32[]{:S(2)}) %collective-permute-start.26) | collective-permute-done | bytes 6176 | tf_op jit(solution)/shard_map/ppermute | solution.py:57
  288.4 5.2 %collective-permute-done.31.low = bf16[384,384]{1,0:T(8,128)(2,1)S(1)} collective-permute-done((bf16[384,384]{1,0:T(8,128)(2,1)S(1)}, bf16[384,384]{1,0:T(8,128)(2,1)S(1)}, u32[]{:S(2)}, u32[]{:S(2)}) %collective-permute-start.31) | collective-permute-done | bytes 294944 | tf_op jit(solution)/shard_map/ppermute | solution.py:61
  294.3 9.8 %table_sum.1 = bf16[4,224,384]{2,1,0:T(8,128)(2,1)S(1)} custom-call(s32[3]{0:T(128)S(1)} %copy-done.21, s32[8,1,768]{2,1,0:T(1,128)S(1)} %compare_select_fusion.3.ids, bf16[2,384,384]{2,1,0:T(8,128)(2,1)S(1)} %pad_maximum_fusion.3.own, bf16[2,384,384]{2,1,0:T(8,128)(2,1)S(1)} %collective-permute-done.29.from_x, ...), custom_call_target="tpu_custom_call" | custom-call | flops 4227858432 | bytes 3072000 | tf_op jit(solution)/shard_map/table_sum/pallas_call | solution.py:36
  307.9 2.9 fusion
  312.2 6.0 %collective-permute-done.34 = bf16[224,384]{1,0:T(8,128)(2,1)S(1)} collective-permute-done((bf16[224,384]{1,0:T(8,128)(2,1)S(1)}, bf16[224,384]{1,0:T(8,128)(2,1)S(1)}, u32[]{:S(2)}, u32[]{:S(2)}) %collective-permute-start.34) | collective-permute-done | bytes 172064 | tf_op jit(solution)/shard_map/ppermute | solution.py:69
  318.1 4.5 collective-permute-done.35
  323.4 8.6 %collective-permute-done.36 = bf16[224,384]{1,0:T(8,128)(2,1)} collective-permute-done((bf16[224,384]{1,0:T(8,128)(2,1)S(1)}, bf16[224,384]{1,0:T(8,128)(2,1)}, u32[]{:S(2)}, u32[]{:S(2)}) %collective-permute-start.36) | collective-permute-done | bytes 172064 | tf_op jit(solution)/shard_map/ppermute | solution.py:57
  337.1 19.5 %collective-permute-done.43 = bf16[2,2,64,1536]{3,2,1,0:T(8,128)(2,1)S(1)} collective-permute-done((bf16[2,2,64,1536]{3,2,1,0:T(8,128)(2,1)S(1)}, bf16[2,2,64,1536]{3,2,1,0:T(8,128)(2,1)S(1)}, u32[]{:S(2)}, u32[]{:S(2)}) %collective-permute-start.43) | collective-permute-done | bytes 786464 | tf_op jit(solution)/shard_map/ppermute | solution.py:61
  357.2 7.8 %collective-permute-done.41 = bf16[2,64,1536]{2,1,0:T(8,128)(2,1)S(1)} collective-permute-done((bf16[2,64,1536]{2,1,0:T(8,128)(2,1)S(1)}, bf16[2,64,1536]{2,1,0:T(8,128)(2,1)S(1)}, u32[]{:S(2)}, u32[]{:S(2)}) %collective-permute-start.41) | collective-permute-done | bytes 393248 | tf_op jit(solution)/shard_map/ppermute | solution.py:61
  365.5 2.8 collective-permute-start.45
  371.1 1.9 collective-permute-start.51
  372.9 4.3 collective-permute-done.45
  377.9 14.5 %collective-permute-done.46 = bf16[64,1536]{1,0:T(8,128)(2,1)S(1)} collective-permute-done((bf16[64,1536]{1,0:T(8,128)(2,1)S(1)}, bf16[64,1536]{1,0:T(8,128)(2,1)S(1)}, u32[]{:S(2)}, u32[]{:S(2)}) %collective-permute-start.46) | collective-permute-done | bytes 196640 | tf_op jit(solution)/shard_map/ppermute | solution.py:69
  393.0 4.1 collective-permute-done.50
  397.1 9.5 %collective-permute-done.51 = bf16[288,512]{1,0:T(8,128)(2,1)S(1)} collective-permute-done((bf16[288,512]{1,0:T(8,128)(2,1)S(1)}, bf16[288,512]{1,0:T(8,128)(2,1)S(1)}, u32[]{:S(2)}, u32[]{:S(2)}) %collective-permute-start.51) | collective-permute-done | bytes 294944 | tf_op jit(solution)/shard_map/ppermute | solution.py:69
  406.6 2.5 collective-permute-done.52
  409.1 1.8 fusion.9
  412.5 3.2 collective-permute-start.38
  415.7 3.3 collective-permute-done.48
  419.0 1.8 select_bitcast_fusion.1
  420.8 1.9 pad_maximum_fusion
  422.8 5.5 %collective-permute-start.49 = (bf16[2,2,64,1536]{3,2,1,0:T(8,128)(2,1)}, bf16[2,2,64,1536]{3,2,1,0:T(8,128)(2,1)}, u32[]{:S(2)}, u32[]{:S(2)}) collective-permute-start(bf16[2,2,64,1536]{3,2,1,0:T(8,128)(2,1)} %pad_maximum_fusion), channel_id=1, source_target_pairs={{0,1},{1,0},{2,3},{3,2},{4,5},{5,4},{6,7},{7,6},{8,9},{9,8},{10,11... | collective-permute-start | bytes 2359304 | tf_op jit(solution)/shard_map/ppermute | solution.py:53
  429.4 2.4 copy.76
  431.9 5.6 %reshape.581 = f32[2,1792,192]{1,2,0:T(8,128)} reshape(f32[2,4,2,224,192]{3,2,1,4,0:T(2,128)S(1)} %copy.76) | data formatting | bytes 5505024 | tf_op jit(solution)/shard_map/convert_element_type | solution.py:696
  448.3 2.0 copy.85
  (307 shorter events, 93.4 us)
Async XLA Ops:
  7.2 138.1 %all-gather.7.cloned.1.call-start = ((), (), s32[]{:S(2)}) async-start(), calls=%async_computation.2 | async-start | bytes 3244032 | tf_op jit(solution)/shard_map/all_gather | solution.py:492
  8.9 151.5 %all-gather.5.cloned.1.call-start = ((), (), s32[]{:S(2)}) async-start(), calls=%async_computation.1 | async-start | bytes 6488064 | tf_op jit(solution)/shard_map/all_gather | solution.py:489
  9.7 358.6 %reduce-scatter.2.cloned.1.call-start = ((), (), s32[]{:S(2)}) async-start(), calls=%async_computation.3 | async-start | bytes 10616832 | tf_op jit(solution)/shard_map/reduce_scatter | solution.py:624
  15.2 18.8 %collective-permute-start.3 = (bf16[264,384]{1,0:T(8,128)(2,1)}, bf16[264,384]{1,0:T(8,128)(2,1)S(1)}, u32[]{:S(2)}, u32[]{:S(2)}) collective-permute-start(bf16[264,384]{1,0:T(8,128)(2,1)} %fusion.18), channel_id=1, source_target_pairs={{24,0},{0,8},{8,16},{16,24},{25,1},{1,9},{9,17},{17,25},{26,2},{2,... | collective-permute-start | bytes 608264 | tf_op jit(solution)/shard_map/ppermute | solution.py:65
  16.5 18.1 %collective-permute-start.1 = (bf16[264,384]{1,0:T(8,128)(2,1)}, bf16[264,384]{1,0:T(8,128)(2,1)}, u32[]{:S(2)}, u32[]{:S(2)}) collective-permute-start(bf16[264,384]{1,0:T(8,128)(2,1)} %fusion.18), channel_id=1, source_target_pairs={{8,0},{16,8},{24,16},{0,24},{9,1},{17,9},{25,17},{1,25},{10,2},{18... | collective-permute-start | bytes 608264 | tf_op jit(solution)/shard_map/ppermute | solution.py:65
  16.7 25.3 %collective-permute-start.2 = (bf16[264,384]{1,0:T(8,128)(2,1)}, bf16[264,384]{1,0:T(8,128)(2,1)}, u32[]{:S(2)}, u32[]{:S(2)}) collective-permute-start(bf16[264,384]{1,0:T(8,128)(2,1)} %fusion.18), channel_id=1, source_target_pairs={{16,0},{24,8},{0,16},{8,24},{17,1},{25,9},{1,17},{9,25},{18,2},{26... | collective-permute-start | bytes 608264 | tf_op jit(solution)/shard_map/ppermute | solution.py:65
  19.1 13.0 %collective-permute-start = (s32[2,768]{1,0:T(2,128)S(1)}, s32[2,768]{1,0:T(2,128)S(1)}, u32[]{:S(2)}, u32[]{:S(2)}) collective-permute-start(s32[2,768]{1,0:T(2,128)S(1)} %bitcast.203), channel_id=1, source_target_pairs={{0,1},{1,0},{2,3},{3,2},{4,5},{5,4},{6,7},{7,6},{8,9},{9,8},{10,11... | collective-permute-start | bytes 18440 | tf_op jit(solution)/shard_map/ppermute | solution.py:53
  23.0 25.0 %collective-permute-start.14 = (bf16[48,1536]{1,0:T(8,128)(2,1)}, bf16[48,1536]{1,0:T(8,128)(2,1)}, u32[]{:S(2)}, u32[]{:S(2)}) collective-permute-start(bf16[48,1536]{1,0:T(8,128)(2,1)} %pad_maximum_fusion.11), channel_id=1, source_target_pairs={{8,0},{16,8},{24,16},{0,24},{9,1},{17,9},{25,17},{1,25},{10,2},{18... | collective-permute-start | bytes 442376 | tf_op jit(solution)/shard_map/ppermute | solution.py:65
  32.1 15.9 %collective-permute-start.15 = (bf16[48,1536]{1,0:T(8,128)(2,1)}, bf16[48,1536]{1,0:T(8,128)(2,1)S(1)}, u32[]{:S(2)}, u32[]{:S(2)}) collective-permute-start(bf16[48,1536]{1,0:T(8,128)(2,1)} %pad_maximum_fusion.11), channel_id=1, source_target_pairs={{16,0},{24,8},{0,16},{8,24},{17,1},{25,9},{1,17},{9,25},{18,2},{26... | collective-permute-start | bytes 442376 | tf_op jit(solution)/shard_map/ppermute | solution.py:65
  34.0 14.3 %collective-permute-start.16 = (bf16[48,1536]{1,0:T(8,128)(2,1)}, bf16[48,1536]{1,0:T(8,128)(2,1)S(1)}, u32[]{:S(2)}, u32[]{:S(2)}) collective-permute-start(bf16[48,1536]{1,0:T(8,128)(2,1)} %pad_maximum_fusion.11), channel_id=1, source_target_pairs={{24,0},{0,8},{8,16},{16,24},{25,1},{1,9},{9,17},{17,25},{26,2},{2,... | collective-permute-start | bytes 442376 | tf_op jit(solution)/shard_map/ppermute | solution.py:65
  43.2 13.9 %collective-permute-start.5 = (bf16[3,264,384]{2,1,0:T(8,128)(2,1)S(1)}, bf16[3,264,384]{2,1,0:T(8,128)(2,1)S(1)}, u32[]{:S(2)}, u32[]{:S(2)}) collective-permute-start(bf16[3,264,384]{2,1,0:T(8,128)(2,1)S(1)} %pad_maximum_fusion.2), channel_id=1, source_target_pairs={{0,4},{1,5},{2,6},{3,7},{4,0},{5,1},{6,2},{7,3},{8,12},{9,13},{10,... | collective-permute-start | bytes 1824776 | tf_op jit(solution)/shard_map/ppermute | solution.py:61
  43.5 15.0 %collective-permute-start.4 = (bf16[3,264,384]{2,1,0:T(8,128)(2,1)S(1)}, bf16[3,264,384]{2,1,0:T(8,128)(2,1)S(1)}, u32[]{:S(2)}, u32[]{:S(2)}) collective-permute-start(bf16[3,264,384]{2,1,0:T(8,128)(2,1)S(1)} %pad_maximum_fusion.2), channel_id=1, source_target_pairs={{0,2},{1,3},{2,0},{3,1},{4,6},{5,7},{6,4},{7,5},{8,10},{9,11},{10,... | collective-permute-start | bytes 1824776 | tf_op jit(solution)/shard_map/ppermute | solution.py:57
  50.1 18.0 %collective-permute-start.17 = (bf16[3,48,1536]{2,1,0:T(8,128)(2,1)}, bf16[3,48,1536]{2,1,0:T(8,128)(2,1)}, u32[]{:S(2)}, u32[]{:S(2)}) collective-permute-start(bf16[3,48,1536]{2,1,0:T(8,128)(2,1)} %pad_maximum_fusion.5.b0), channel_id=1, source_target_pairs={{0,2},{1,3},{2,0},{3,1},{4,6},{5,7},{6,4},{7,5},{8,10},{9,11},{10,... | collective-permute-start | bytes 1327112 | tf_op jit(solution)/shard_map/ppermute | solution.py:57
  51.4 30.8 %collective-permute-start.18 = (bf16[3,48,1536]{2,1,0:T(8,128)(2,1)}, bf16[3,48,1536]{2,1,0:T(8,128)(2,1)}, u32[]{:S(2)}, u32[]{:S(2)}) collective-permute-start(bf16[3,48,1536]{2,1,0:T(8,128)(2,1)} %pad_maximum_fusion.5.b0), channel_id=1, source_target_pairs={{0,4},{1,5},{2,6},{3,7},{4,0},{5,1},{6,2},{7,3},{8,12},{9,13},{10,... | collective-permute-start | bytes 1327112 | tf_op jit(solution)/shard_map/ppermute | solution.py:61
  51.8 43.4 %collective-permute-start.21 = (bf16[3,48,1536]{2,1,0:T(8,128)(2,1)}, bf16[3,48,1536]{2,1,0:T(8,128)(2,1)}, u32[]{:S(2)}, u32[]{:S(2)}) collective-permute-start(bf16[3,48,1536]{2,1,0:T(8,128)(2,1)} %pad_maximum_fusion.5.b0), channel_id=1, source_target_pairs={{0,1},{1,0},{2,3},{3,2},{4,5},{5,4},{6,7},{7,6},{8,9},{9,8},{10,11... | collective-permute-start | bytes 1327112 | tf_op jit(solution)/shard_map/ppermute | solution.py:53
  57.2 28.7 %collective-permute-start.7 = (bf16[3,136,384]{2,1,0:T(8,128)(2,1)S(1)}, bf16[3,136,384]{2,1,0:T(8,128)(2,1)S(1)}, u32[]{:S(2)}, u32[]{:S(2)}) collective-permute-start(bf16[3,136,384]{2,1,0:T(8,128)(2,1)S(1)} %slice.264), channel_id=1, source_target_pairs={{0,2},{1,3},{2,0},{3,1},{4,6},{5,7},{6,4},{7,5},{8,10},{9,11},{10,... | collective-permute-start | bytes 940040 | tf_op jit(solution)/shard_map/ppermute | solution.py:57
  58.6 28.0 %collective-permute-start.6 = (bf16[3,128,384]{2,1,0:T(8,128)(2,1)S(1)}, bf16[3,128,384]{2,1,0:T(8,128)(2,1)S(1)}, u32[]{:S(2)}, u32[]{:S(2)}) collective-permute-start(bf16[3,128,384]{2,1,0:T(8,128)(2,1)S(1)} %slice.263), channel_id=1, source_target_pairs={{0,4},{1,5},{2,6},{3,7},{4,0},{5,1},{6,2},{7,3},{8,12},{9,13},{10,... | collective-permute-start | bytes 884744 | tf_op jit(solution)/shard_map/ppermute | solution.py:61
  68.1 26.5 %collective-permute-start.9 = (bf16[3,32,384]{2,1,0:T(8,128)(2,1)}, bf16[3,32,384]{2,1,0:T(8,128)(2,1)}, u32[]{:S(2)}, u32[]{:S(2)}) collective-permute-start(bf16[3,32,384]{2,1,0:T(8,128)(2,1)} %slice.275), channel_id=1, source_target_pairs={{0,1},{1,0},{2,3},{3,2},{4,5},{5,4},{6,7},{7,6},{8,9},{9,8},{10,11... | collective-permute-start | bytes 221192 | tf_op jit(solution)/shard_map/ppermute | solution.py:53
  82.2 13.2 %collective-permute-start.19 = (bf16[3,48,768]{2,1,0:T(8,128)(2,1)}, bf16[3,48,768]{2,1,0:T(8,128)(2,1)}, u32[]{:S(2)}, u32[]{:S(2)}) collective-permute-start(bf16[3,48,768]{2,1,0:T(8,128)(2,1)} %slice.280), channel_id=1, source_target_pairs={{0,4},{1,5},{2,6},{3,7},{4,0},{5,1},{6,2},{7,3},{8,12},{9,13},{10,... | collective-permute-start | bytes 663560 | tf_op jit(solution)/shard_map/ppermute | solution.py:61
  85.9 10.8 %collective-permute-start.20 = (bf16[3,48,768]{2,1,0:T(8,128)(2,1)}, bf16[3,48,768]{2,1,0:T(8,128)(2,1)}, u32[]{:S(2)}, u32[]{:S(2)}) collective-permute-start(bf16[3,48,768]{2,1,0:T(8,128)(2,1)} %slice.281), channel_id=1, source_target_pairs={{0,2},{1,3},{2,0},{3,1},{4,6},{5,7},{6,4},{7,5},{8,10},{9,11},{10,... | collective-permute-start | bytes 663560 | tf_op jit(solution)/shard_map/ppermute | solution.py:57
  86.6 17.1 %collective-permute-start.22 = (bf16[3,48,1536]{2,1,0:T(8,128)(2,1)}, bf16[3,48,1536]{2,1,0:T(8,128)(2,1)}, u32[]{:S(2)}, u32[]{:S(2)}) collective-permute-start(bf16[3,48,1536]{2,1,0:T(8,128)(2,1)} %collective-permute-done.17.bx), channel_id=1, source_target_pairs={{0,1},{1,0},{2,3},{3,2},{4,5},{5,4},{6,7},{7,6},{8,9},{9,8},{10,11... | collective-permute-start | bytes 1327112 | tf_op jit(solution)/shard_map/ppermute | solution.py:53
  94.6 9.1 %collective-permute-start.23 = (bf16[3,48,1536]{2,1,0:T(8,128)(2,1)}, bf16[3,48,1536]{2,1,0:T(8,128)(2,1)}, u32[]{:S(2)}, u32[]{:S(2)}) collective-permute-start(bf16[3,48,1536]{2,1,0:T(8,128)(2,1)} %collective-permute-done.18.by), channel_id=1, source_target_pairs={{0,1},{1,0},{2,3},{3,2},{4,5},{5,4},{6,7},{7,6},{8,9},{9,8},{10,11... | collective-permute-start | bytes 1327112 | tf_op jit(solution)/shard_map/ppermute | solution.py:53
  97.3 6.5 %collective-permute-start.8 = (bf16[768,192]{1,0:T(8,128)(2,1)}, bf16[768,192]{1,0:T(8,128)(2,1)S(1)}, u32[]{:S(2)}, u32[]{:S(2)}) collective-permute-start(bf16[768,192]{1,0:T(8,128)(2,1)} %get-tuple-element.109), channel_id=1, source_target_pairs={{0,1},{1,0},{2,3},{3,2},{4,5},{5,4},{6,7},{7,6},{8,9},{9,8},{10,11... | collective-permute-start | bytes 884744 | tf_op jit(solution)/shard_map/ppermute | solution.py:53
  199.4 245.6 %all-gather.9.cloned.1.call-start = ((), (), s32[]{:S(2)}) async-start(), calls=%async_computation.4 | async-start | bytes 2654208 | tf_op jit(solution)/shard_map/all_gather | solution.py:693
  255.5 52.3 %collective-permute-start.39 = (bf16[4,4,64,1536]{3,2,1,0:T(8,128)(2,1)}, bf16[4,4,64,1536]{3,2,1,0:T(8,128)(2,1)}, u32[]{:S(2)}, u32[]{:S(2)}) collective-permute-start(bf16[4,4,64,1536]{3,2,1,0:T(8,128)(2,1)} %slice_bitcast_fusion.1), channel_id=1, source_target_pairs={{0,1},{1,0},{2,3},{3,2},{4,5},{5,4},{6,7},{7,6},{8,9},{9,8},{10,11... | collective-permute-start | bytes 9437192 | tf_op jit(solution)/shard_map/ppermute | solution.py:53
  261.7 23.9 %collective-permute-start.29 = (bf16[2,384,384]{2,1,0:T(8,128)(2,1)S(1)}, bf16[2,384,384]{2,1,0:T(8,128)(2,1)S(1)}, u32[]{:S(2)}, u32[]{:S(2)}) collective-permute-start(bf16[2,384,384]{2,1,0:T(8,128)(2,1)S(1)} %pad_maximum_fusion.3.own), channel_id=1, source_target_pairs={{0,2},{1,3},{2,0},{3,1},{4,6},{5,7},{6,4},{7,5},{8,10},{9,11},{10,... | collective-permute-start | bytes 1769480 | tf_op jit(solution)/shard_map/ppermute | solution.py:57
  261.7 25.1 %collective-permute-start.30 = (bf16[2,384,384]{2,1,0:T(8,128)(2,1)S(1)}, bf16[2,384,384]{2,1,0:T(8,128)(2,1)S(1)}, u32[]{:S(2)}, u32[]{:S(2)}) collective-permute-start(bf16[2,384,384]{2,1,0:T(8,128)(2,1)S(1)} %pad_maximum_fusion.3.own), channel_id=1, source_target_pairs={{0,4},{1,5},{2,6},{3,7},{4,0},{5,1},{6,2},{7,3},{8,12},{9,13},{10,... | collective-permute-start | bytes 1769480 | tf_op jit(solution)/shard_map/ppermute | solution.py:61
  263.0 22.3 %collective-permute-start.26 = (s32[2,768]{1,0:T(2,128)S(1)}, s32[2,768]{1,0:T(2,128)S(1)}, u32[]{:S(2)}, u32[]{:S(2)}) collective-permute-start(s32[2,768]{1,0:T(2,128)S(1)} %copy-done.37), channel_id=1, source_target_pairs={{0,2},{1,3},{2,0},{3,1},{4,6},{5,7},{6,4},{7,5},{8,10},{9,11},{10,... | collective-permute-start | bytes 18440 | tf_op jit(solution)/shard_map/ppermute | solution.py:57
  285.6 8.0 %collective-permute-start.31 = (bf16[384,384]{1,0:T(8,128)(2,1)S(1)}, bf16[384,384]{1,0:T(8,128)(2,1)S(1)}, u32[]{:S(2)}, u32[]{:S(2)}) collective-permute-start(bf16[384,384]{1,0:T(8,128)(2,1)S(1)} %slice_bitcast_fusion.15), channel_id=1, source_target_pairs={{0,4},{1,5},{2,6},{3,7},{4,0},{5,1},{6,2},{7,3},{8,12},{9,13},{10,... | collective-permute-start | bytes 884744 | tf_op jit(solution)/shard_map/ppermute | solution.py:61
  286.9 7.4 %collective-permute-start.32 = (bf16[384,384]{1,0:T(8,128)(2,1)S(1)}, bf16[384,384]{1,0:T(8,128)(2,1)S(1)}, u32[]{:S(2)}, u32[]{:S(2)}) collective-permute-start(bf16[384,384]{1,0:T(8,128)(2,1)S(1)} %slice_bitcast_fusion.14), channel_id=1, source_target_pairs={{0,2},{1,3},{2,0},{3,1},{4,6},{5,7},{6,4},{7,5},{8,10},{9,11},{10,... | collective-permute-start | bytes 884744 | tf_op jit(solution)/shard_map/ppermute | solution.py:57
  304.2 8.0 %collective-permute-start.33 = (bf16[224,384]{1,0:T(8,128)(2,1)S(1)}, bf16[224,384]{1,0:T(8,128)(2,1)S(1)}, u32[]{:S(2)}, u32[]{:S(2)}) collective-permute-start(bf16[224,384]{1,0:T(8,128)(2,1)S(1)} %get-tuple-element.115), channel_id=1, source_target_pairs={{0,8},{8,16},{16,24},{24,0},{1,9},{9,17},{17,25},{25,1},{2,10},{10... | collective-permute-start | bytes 516104 | tf_op jit(solution)/shard_map/ppermute | solution.py:69
  305.3 12.8 %collective-permute-start.34 = (bf16[224,384]{1,0:T(8,128)(2,1)S(1)}, bf16[224,384]{1,0:T(8,128)(2,1)S(1)}, u32[]{:S(2)}, u32[]{:S(2)}) collective-permute-start(bf16[224,384]{1,0:T(8,128)(2,1)S(1)} %get-tuple-element.117), channel_id=1, source_target_pairs={{0,16},{8,24},{16,0},{24,8},{1,17},{9,25},{17,1},{25,9},{2,18},{10... | collective-permute-start | bytes 516104 | tf_op jit(solution)/shard_map/ppermute | solution.py:69
  306.6 16.0 %collective-permute-start.35 = (bf16[224,384]{1,0:T(8,128)(2,1)S(1)}, bf16[224,384]{1,0:T(8,128)(2,1)S(1)}, u32[]{:S(2)}, u32[]{:S(2)}) collective-permute-start(bf16[224,384]{1,0:T(8,128)(2,1)S(1)} %get-tuple-element.116), channel_id=1, source_target_pairs={{0,24},{8,0},{16,8},{24,16},{1,25},{9,1},{17,9},{25,17},{2,26},{10... | collective-permute-start | bytes 516104 | tf_op jit(solution)/shard_map/ppermute | solution.py:69
  311.9 23.5 %collective-permute-start.40 = (bf16[2,2,64,1536]{3,2,1,0:T(8,128)(2,1)}, bf16[2,2,64,1536]{3,2,1,0:T(8,128)(2,1)}, u32[]{:S(2)}, u32[]{:S(2)}) collective-permute-start(bf16[2,2,64,1536]{3,2,1,0:T(8,128)(2,1)} %slice.231), channel_id=1, source_target_pairs={{0,2},{1,3},{2,0},{3,1},{4,6},{5,7},{6,4},{7,5},{8,10},{9,11},{10,... | collective-permute-start | bytes 2359304 | tf_op jit(solution)/shard_map/ppermute | solution.py:57
  322.8 9.2 %collective-permute-start.36 = (bf16[224,384]{1,0:T(8,128)(2,1)S(1)}, bf16[224,384]{1,0:T(8,128)(2,1)}, u32[]{:S(2)}, u32[]{:S(2)}) collective-permute-start(bf16[224,384]{1,0:T(8,128)(2,1)S(1)} %fusion.16), channel_id=1, source_target_pairs={{0,2},{1,3},{2,0},{3,1},{4,6},{5,7},{6,4},{7,5},{8,10},{9,11},{10,... | collective-permute-start | bytes 516104 | tf_op jit(solution)/shard_map/ppermute | solution.py:57
  333.8 77.5 %collective-permute-start.37 = (bf16[2,224,384]{2,1,0:T(8,128)(2,1)}, bf16[2,224,384]{2,1,0:T(8,128)(2,1)}, u32[]{:S(2)}, u32[]{:S(2)}) collective-permute-start(bf16[2,224,384]{2,1,0:T(8,128)(2,1)} %pad_maximum_fusion.9), channel_id=1, source_target_pairs={{0,4},{1,5},{2,6},{3,7},{4,0},{5,1},{6,2},{7,3},{8,12},{9,13},{10,... | collective-permute-start | bytes 1032200 | tf_op jit(solution)/shard_map/ppermute | solution.py:61
  334.2 22.4 %collective-permute-start.43 = (bf16[2,2,64,1536]{3,2,1,0:T(8,128)(2,1)S(1)}, bf16[2,2,64,1536]{3,2,1,0:T(8,128)(2,1)S(1)}, u32[]{:S(2)}, u32[]{:S(2)}) collective-permute-start(bf16[2,2,64,1536]{3,2,1,0:T(8,128)(2,1)S(1)} %slice.297), channel_id=1, source_target_pairs={{0,4},{1,5},{2,6},{3,7},{4,0},{5,1},{6,2},{7,3},{8,12},{9,13},{10,... | collective-permute-start | bytes 2359304 | tf_op jit(solution)/shard_map/ppermute | solution.py:61
  336.8 28.2 %collective-permute-start.41 = (bf16[2,64,1536]{2,1,0:T(8,128)(2,1)S(1)}, bf16[2,64,1536]{2,1,0:T(8,128)(2,1)S(1)}, u32[]{:S(2)}, u32[]{:S(2)}) collective-permute-start(bf16[2,64,1536]{2,1,0:T(8,128)(2,1)S(1)} %slice_bitcast_fusion.6), channel_id=1, source_target_pairs={{0,4},{1,5},{2,6},{3,7},{4,0},{5,1},{6,2},{7,3},{8,12},{9,13},{10,... | collective-permute-start | bytes 1179656 | tf_op jit(solution)/shard_map/ppermute | solution.py:61
  356.8 8.6 %collective-permute-start.44 = (bf16[2,64,1536]{2,1,0:T(8,128)(2,1)S(1)}, bf16[2,64,1536]{2,1,0:T(8,128)(2,1)S(1)}, u32[]{:S(2)}, u32[]{:S(2)}) collective-permute-start(bf16[2,64,1536]{2,1,0:T(8,128)(2,1)S(1)} %slice_bitcast_fusion.4), channel_id=1, source_target_pairs={{0,2},{1,3},{2,0},{3,1},{4,6},{5,7},{6,4},{7,5},{8,10},{9,11},{10,... | collective-permute-start | bytes 1179656 | tf_op jit(solution)/shard_map/ppermute | solution.py:57
  365.5 11.7 %collective-permute-start.45 = (bf16[64,1536]{1,0:T(8,128)(2,1)S(1)}, bf16[64,1536]{1,0:T(8,128)(2,1)S(1)}, u32[]{:S(2)}, u32[]{:S(2)}) collective-permute-start(bf16[64,1536]{1,0:T(8,128)(2,1)S(1)} %get-tuple-element.122), channel_id=1, source_target_pairs={{0,16},{8,24},{16,0},{24,8},{1,17},{9,25},{17,1},{25,9},{2,18},{10... | collective-permute-start | bytes 589832 | tf_op jit(solution)/shard_map/ppermute | solution.py:69
  368.3 24.1 %collective-permute-start.46 = (bf16[64,1536]{1,0:T(8,128)(2,1)S(1)}, bf16[64,1536]{1,0:T(8,128)(2,1)S(1)}, u32[]{:S(2)}, u32[]{:S(2)}) collective-permute-start(bf16[64,1536]{1,0:T(8,128)(2,1)S(1)} %get-tuple-element.123), channel_id=1, source_target_pairs={{0,24},{8,0},{16,8},{24,16},{1,25},{9,1},{17,9},{25,17},{2,26},{10... | collective-permute-start | bytes 589832 | tf_op jit(solution)/shard_map/ppermute | solution.py:69
  369.5 27.5 %collective-permute-start.50 = (bf16[288,512]{1,0:T(8,128)(2,1)S(1)}, bf16[288,512]{1,0:T(8,128)(2,1)S(1)}, u32[]{:S(2)}, u32[]{:S(2)}) collective-permute-start(bf16[288,512]{1,0:T(8,128)(2,1)S(1)} %get-tuple-element.104), channel_id=1, source_target_pairs={{0,8},{8,16},{16,24},{24,0},{1,9},{9,17},{17,25},{25,1},{2,10},{10... | collective-permute-start | bytes 884744 | tf_op jit(solution)/shard_map/ppermute | solution.py:69
  371.1 35.5 %collective-permute-start.51 = (bf16[288,512]{1,0:T(8,128)(2,1)S(1)}, bf16[288,512]{1,0:T(8,128)(2,1)S(1)}, u32[]{:S(2)}, u32[]{:S(2)}) collective-permute-start(bf16[288,512]{1,0:T(8,128)(2,1)S(1)} %get-tuple-element.106), channel_id=1, source_target_pairs={{0,16},{8,24},{16,0},{24,8},{1,17},{9,25},{17,1},{25,9},{2,18},{10... | collective-permute-start | bytes 884744 | tf_op jit(solution)/shard_map/ppermute | solution.py:69
  377.3 31.8 %collective-permute-start.52 = (bf16[288,512]{1,0:T(8,128)(2,1)S(1)}, bf16[288,512]{1,0:T(8,128)(2,1)S(1)}, u32[]{:S(2)}, u32[]{:S(2)}) collective-permute-start(bf16[288,512]{1,0:T(8,128)(2,1)S(1)} %get-tuple-element.105), channel_id=1, source_target_pairs={{0,24},{8,0},{16,8},{24,16},{1,25},{9,1},{17,9},{25,17},{2,26},{10... | collective-permute-start | bytes 884744 | tf_op jit(solution)/shard_map/ppermute | solution.py:69
  392.5 18.4 %collective-permute-start.47 = (bf16[64,1536]{1,0:T(8,128)(2,1)S(1)}, bf16[64,1536]{1,0:T(8,128)(2,1)S(1)}, u32[]{:S(2)}, u32[]{:S(2)}) collective-permute-start(bf16[64,1536]{1,0:T(8,128)(2,1)S(1)} %fusion.13), channel_id=1, source_target_pairs={{0,2},{1,3},{2,0},{3,1},{4,6},{5,7},{6,4},{7,5},{8,10},{9,11},{10,... | collective-permute-start | bytes 589832 | tf_op jit(solution)/shard_map/ppermute | solution.py:57
  411.0 8.0 %collective-permute-start.48 = (bf16[2,64,1536]{2,1,0:T(8,128)(2,1)S(1)}, bf16[2,64,1536]{2,1,0:T(8,128)(2,1)}, u32[]{:S(2)}, u32[]{:S(2)}) collective-permute-start(bf16[2,64,1536]{2,1,0:T(8,128)(2,1)S(1)} %pad_maximum_fusion.8), channel_id=1, source_target_pairs={{0,4},{1,5},{2,6},{3,7},{4,0},{5,1},{6,2},{7,3},{8,12},{9,13},{10,... | collective-permute-start | bytes 1179656 | tf_op jit(solution)/shard_map/ppermute | solution.py:61
  412.5 15.8 %collective-permute-start.38 = (bf16[2,2,224,384]{3,2,1,0:T(8,128)(2,1)S(1)}, bf16[2,2,224,384]{3,2,1,0:T(8,128)(2,1)S(1)}, u32[]{:S(2)}, u32[]{:S(2)}) collective-permute-start(bf16[2,2,224,384]{3,2,1,0:T(8,128)(2,1)S(1)} %pad_maximum_fusion.1), channel_id=1, source_target_pairs={{0,1},{1,0},{2,3},{3,2},{4,5},{5,4},{6,7},{7,6},{8,9},{9,8},{10,11... | collective-permute-start | bytes 2064392 | tf_op jit(solution)/shard_map/ppermute | solution.py:53
  422.8 14.7 %collective-permute-start.49 = (bf16[2,2,64,1536]{3,2,1,0:T(8,128)(2,1)}, bf16[2,2,64,1536]{3,2,1,0:T(8,128)(2,1)}, u32[]{:S(2)}, u32[]{:S(2)}) collective-permute-start(bf16[2,2,64,1536]{3,2,1,0:T(8,128)(2,1)} %pad_maximum_fusion), channel_id=1, source_target_pairs={{0,1},{1,0},{2,3},{3,2},{4,5},{5,4},{6,7},{7,6},{8,9},{9,8},{10,11... | collective-permute-start | bytes 2359304 | tf_op jit(solution)/shard_map/ppermute | solution.py:53
  (59 other events, 401.6 us)
Sparse Core Ops, SparseCore 0:
  10.9 78.7 all-gather.6
  92.5 67.8 all-gather.4
  199.5 82.3 reduce-scatter.1
  411.0 29.8 all-gather.8
